TPU v7x, 32 devices: a whole 2x2x4 slice. The times are simulated.
32 devices in a mesh: pos: 4 (over x, core), head: 4 (over z), chan: 2 (over y).
Axes of the slice: x: 2, y: 2, z: 4, core: 2. Of those that a mesh axis runs over, the one named last changes fastest.
Arguments:
- inputs_saved: bfloat16 [3, 8192, 1536], P(None, ('pos', 'head'), 'chan'), may hold values from -6 to 6
- conv_weight: bfloat16 [3, 3, 1536, 768], P(None, None, 'chan'), may hold values from -0.09375 to 0.09375
- expand_weight: bfloat16 [3, 768, 1536], P(None, None, 'chan'), may hold values from -0.21875 to 0.21875
- head_weight: bfloat16 [1024, 1536], P(('pos', 'head')), may hold values from -1.796875 to 1.796875
- batch_of: int32 [1024], P(('pos', 'head')), may hold values from 0 to 7
- erase_left: bfloat16 [1536, 64], replicated, may hold values from -0.15625 to 0.15625
- erase_right: bfloat16 [1536, 64], replicated, may hold values from -2.09375 to 2.09375
- bin_gradient: bfloat16 [1024, 32], P(('pos', 'head')), may hold values from -6 to 6
- cover_bins: int32 [1024, 32], P(('pos', 'head')), may hold values from 0 to 8191, as said below
Outputs:
- input_grad: bfloat16 [8192, 1536], P(('pos', 'head'), 'chan')
Inputs may be any that keep to these rules, and one draw needn't show every extreme that they name: `cover_bins`: of the 2048 entries of the experiments held by one device of pos and head, at most 256 name positions of any one device; in every draw some device's positions are named by exactly 256 entries of every device. Positions may repeat within an experiment.
All inputs are finite; a program needn't handle non-finite values.
Results may differ from a plain program's by a relative error of at most 0.0095.
Values may be sent and summed in bfloat16 or wider, within the bound.
A program may use at most 128 MiB of HBM per device.

v0:
```python
import jax
import jax.numpy as jnp
from jax import lax
from jax.sharding import PartitionSpec as P

BASE_DILATION = 4
RANK = 8


def with_halo(block, sides, width):
    for axis, dim in sides:
        count = lax.axis_size(axis)
        forward = [(i, i + 1) for i in range(count - 1)]
        backward = [(target, source) for source, target in forward]
        low = lax.ppermute(
            lax.slice_in_dim(block, block.shape[dim] - width, None, axis=dim), axis, forward
        )
        high = lax.ppermute(lax.slice_in_dim(block, 0, width, axis=dim), axis, backward)
        block = jnp.concatenate([low, block, high], axis=dim)
    return block


def gelu_value(value):
    return 0.5 * value * (1.0 + jax.scipy.special.erf(value * 0.7071067811865476))


def gelu_slope(value):
    return (
        0.5 * (1.0 + jax.scipy.special.erf(value * 0.7071067811865476))
        + value * jnp.exp(-0.5 * value * value) * 0.3989422804014327
    )


def per_device(
    inputs_saved,
    conv_weight,
    expand_weight,
    head_weight,
    batch_of,
    erase_left,
    erase_right,
    bin_gradient,
    cover_bins,
):
    members = lax.axis_size(("pos", "head"))
    width_share = inputs_saved.shape[2]
    local_rows = inputs_saved.shape[1]
    exp_local = head_weight.shape[0]
    cover_count = bin_gradient.shape[1]
    chan_place = lax.axis_index("chan")
    projected = jnp.dot(head_weight, erase_left, preferred_element_type=jnp.float32)
    columns = jnp.arange(erase_left.shape[1]) // RANK
    chosen = (columns[None, :] == batch_of[:, None]).astype(jnp.float32)
    right_share = lax.dynamic_slice_in_dim(erase_right, chan_place * width_share, width_share, 0)
    weight_share = lax.dynamic_slice_in_dim(head_weight, chan_place * width_share, width_share, 1)
    removed_rows = jnp.dot(
        projected * chosen, right_share.astype(jnp.float32).T, precision=lax.Precision.HIGHEST
    )
    vectors = (weight_share.astype(jnp.float32) - removed_rows).astype(jnp.bfloat16)
    entry_list = exp_local * cover_count
    flat_bins = cover_bins.reshape(-1)
    flat_grad = bin_gradient.reshape(-1).astype(jnp.float32)
    target = flat_bins // local_rows
    offset = flat_bins % local_rows
    capacity = 2 * entry_list // members
    one_hot = (target[:, None] == jnp.arange(members)[None, :]).astype(jnp.int32)
    ranking = jnp.sum((jnp.cumsum(one_hot, axis=0) - 1) * one_hot, axis=1)
    slot_index = target * capacity + ranking
    owner = (
        jnp.full((members * capacity,), -1, jnp.int32)
        .at[slot_index]
        .set(jnp.arange(entry_list, dtype=jnp.int32))
    )
    filled = owner >= 0
    source = jnp.maximum(owner, 0)
    slot_weight = jnp.where(filled, flat_grad[source], 0.0)
    slot_place = jnp.where(filled, offset[source], 0).astype(jnp.float32)
    local_exp = source // cover_count
    contrib = slot_weight[:, None] * vectors[local_exp].astype(jnp.float32)
    got_values, got_place = (
        lax.all_to_all(
            contrib.reshape(members, capacity, width_share),
            ("pos", "head"),
            split_axis=0,
            concat_axis=0,
            tiled=True,
        ),
        lax.all_to_all(
            slot_place.reshape(members, capacity),
            ("pos", "head"),
            split_axis=0,
            concat_axis=0,
            tiled=True,
        ),
    )
    flat_values = got_values.reshape(-1, width_share)
    grad = jax.ops.segment_sum(
        flat_values, got_place.reshape(-1).astype(jnp.int32), num_segments=local_rows
    )
    taps = conv_weight.shape[1]
    layer_count = inputs_saved.shape[0]
    for block_level in reversed(range(layer_count)):
        dilation_factor = BASE_DILATION * 2**block_level
        saved = inputs_saved[block_level].astype(jnp.float32)
        act = gelu_value(saved).astype(jnp.bfloat16)
        act_pad = with_halo(act, ((("pos", "head"), 0),), dilation_factor)
        partial_result = jnp.zeros((local_rows, conv_weight.shape[3]), jnp.float32)
        for kernel_tap in range(taps):
            start = kernel_tap * dilation_factor
            partial_result = partial_result + jnp.dot(
                act_pad[start : start + local_rows],
                conv_weight[block_level, kernel_tap],
                preferred_element_type=jnp.float32,
            )
        grad_in = grad.astype(jnp.bfloat16)
        mid_part = lax.dot_general(
            grad_in,
            expand_weight[block_level],
            (((1,), (1,)), ((), ())),
            preferred_element_type=jnp.float32,
        )
        preceding_sum, mid_sum = lax.psum((partial_result, mid_part), "chan")
        grad_pre = (mid_sum * gelu_slope(preceding_sum)).astype(jnp.bfloat16)
        grad_pad = with_halo(grad_pre, ((("pos", "head"), 0),), dilation_factor)
        grad_act = jnp.zeros((local_rows, width_share), jnp.float32)
        for kernel_tap in range(taps):
            start = (taps - 1 - kernel_tap) * dilation_factor
            grad_act = grad_act + lax.dot_general(
                grad_pad[start : start + local_rows],
                conv_weight[block_level, kernel_tap],
                (((1,), (1,)), ((), ())),
                preferred_element_type=jnp.float32,
            )
        grad = grad + grad_act * gelu_slope(saved)
    return grad.astype(jnp.bfloat16)


def solution(mesh):
    return jax.shard_map(
        per_device,
        mesh=mesh,
        in_specs=(
            P(None, ("pos", "head"), "chan"),
            P(None, None, "chan", None),
            P(None, None, "chan"),
            P(("pos", "head"), None),
            P(("pos", "head")),
            P(),
            P(),
            P(("pos", "head"), None),
            P(("pos", "head"), None),
        ),
        out_specs=P(("pos", "head"), "chan"),
        check_vma=False,
    )
```

profile of v0, /device:TPU:0, one launch (start us, length us, event | category | flops | bytes accessed | tf_op | source)
XLA Modules:
  0.0 744.0 jit_solution(2120107413479196897)
XLA Ops:
  8.5 4.5 reduce-window.6
  13.9 8.1 %scatter_custom_fusion = s32[4096]{0:T(1024)S(1)} fusion(s32[2048]{0:T(1024)S(1)} %bitcast.223, s32[2048]{0:T(1024)S(1)} %iota.16, s32[]{:T(128)} %constant.77.clone.1), kind=kCustom, calls=%fused_computation.240 | custom fusion | bytes 16388 | tf_op jit(solution)/shard_map/scatter | solution.py:72
  22.0 23.0 %gather_fusion.1 = f32[4096]{0:T(1024)S(1)} fusion(f32[2048]{0:T(1024)S(1)} %reshape.188, s32[4096]{0:T(1024)S(1)} %get-tuple-element.29), kind=kCustom, calls=%fused_computation.1 | custom fusion | bytes 49152 | tf_op jit(solution)/shard_map/gather | solution.py:76
  45.1 23.0 %gather_fusion = s32[4096]{0:T(1024)S(1)} fusion(s32[2048]{0:T(1024)S(1)} %get-tuple-element.30, s32[4096]{0:T(1024)S(1)} %get-tuple-element.29), kind=kCustom, calls=%fused_computation | custom fusion | bytes 49152 | tf_op jit(solution)/shard_map/gather | solution.py:77
  68.8 7.4 all-to-all-start
  76.6 17.8 %gather_fusion.2 = bf16[4096,768]{1,0:T(8,128)(2,1)} fusion(bf16[64,768]{1,0:T(8,128)(2,1)S(1)} %fusion.130, s32[4096]{0:T(1024)S(1)} %get-tuple-element.28), kind=kCustom, calls=%fused_computation.2 | custom fusion | bytes 12599296 | tf_op jit(solution)/shard_map/gather | solution.py:79
  94.4 8.3 %convert_multiply_fusion = f32[16,256,768]{2,1,0:T(8,128)} fusion(bf16[16,256,768]{2,1,0:T(8,128)(2,1)} %bitcast.218, f32[16,256]{1,0:T(8,128)S(1)} %mul.211), kind=kLoop, calls=%fused_computation.5 | loop fusion | flops 6291456 | bytes 18890752 | tf_op jit(solution)/shard_map/mul | solution.py:79
  102.7 6.0 all-to-all-start.1
  108.8 2.9 fusion.60
  111.8 3.8 collective-permute-start
  115.5 1.3 collective-permute-start.1
  116.8 2.4 fusion.119
  119.3 193.7 %collective-permute-done = bf16[16,768]{1,0:T(8,128)(2,1)S(1)} collective-permute-done((bf16[16,768]{1,0:T(8,128)(2,1)S(1)}, bf16[16,768]{1,0:T(8,128)(2,1)S(1)}, u32[]{:S(2)}, u32[]{:S(2)}) %collective-permute-start) | collective-permute-done | bytes 24608 | tf_op jit(solution)/shard_map/ppermute | solution.py:15
  312.9 2.1 fusion.123
  315.0 3.3 add_add_fusion.2
  318.3 64.9 %all-to-all-done.1 = f32[16,256,768]{2,1,0:T(8,128)} async-done(((f32[16,256,768]{2,1,0:T(8,128)}), f32[16,256,768]{2,1,0:T(8,128)}, u32[]{:S(2)}, u32[]{:S(2)}) %all-to-all-start.1) | async-done | bytes 12582944 | tf_op jit(solution)/shard_map/all_to_all | solution.py:81
  383.2 29.0 %scatter_custom_fusion.1 = f32[512,768]{1,0:T(8,128)S(1)} fusion(s32[4096]{0:T(1024)S(1)} %bitcast.222, f32[4096,768]{1,0:T(8,128)} %bitcast.6, f32[]{:T(128)} %constant.76.clone.1), kind=kCustom, calls=%fused_computation.199 | custom fusion | flops 3145728 | bytes 1573376 | tf_op jit(solution)/shard_map/scatter-add | solution.py:97
  412.2 3.3 fusion.125
  415.6 6.2 collective-permute-start.4
  421.8 1.5 collective-permute-start.5
  423.3 2.5 fusion.101
  425.8 2.2 fusion.105
  428.0 3.2 add_add_fusion.1
  431.2 74.2 %all-reduce.11.cloned.1.call-done = (f32[512,768]{1,0:T(8,128)}, f32[512,768]{1,0:T(8,128)}) async-done(((f32[512,768]{1,0:T(8,128)}, f32[512,768]{1,0:T(8,128)}), (f32[512,768]{1,0:T(8,128)}, f32[512,768]{1,0:T(8,128)})) %all-reduce.11.cloned.1.call-update) | async-done | bytes 3145744 | tf_op jit(solution)/shard_map/psum | solution.py:122
  505.5 2.5 fusion.20
  509.3 2.1 fusion.117
  511.4 4.5 collective-permute-start.3
  516.0 2.1 fusion.121
  518.1 2.8 fusion.41
  522.0 3.4 fusion.107
  525.5 3.7 collective-permute-start.8
  530.5 2.2 fusion.83
  532.7 2.4 fusion.87
  535.1 3.2 add_add_fusion
  538.4 75.2 %all-reduce.9.cloned.1.call-done = (f32[512,768]{1,0:T(8,128)}, f32[512,768]{1,0:T(8,128)}) async-done(((f32[512,768]{1,0:T(8,128)}, f32[512,768]{1,0:T(8,128)}), (f32[512,768]{1,0:T(8,128)}, f32[512,768]{1,0:T(8,128)})) %all-reduce.9.cloned.1.call-update) | async-done | bytes 3145744 | tf_op jit(solution)/shard_map/psum | solution.py:122
  613.5 2.5 fusion.26
  616.1 1.3 collective-permute-start.6
  617.4 2.1 fusion.99
  619.5 4.9 collective-permute-start.7
  624.4 2.1 fusion.103
  626.5 2.5 fusion.54
  630.2 3.3 fusion.89
  633.5 87.6 %all-reduce.7.cloned.1.call-done = (f32[512,768]{1,0:T(8,128)}, f32[512,768]{1,0:T(8,128)}) async-done(((f32[512,768]{1,0:T(8,128)}, f32[512,768]{1,0:T(8,128)}), (f32[512,768]{1,0:T(8,128)}, f32[512,768]{1,0:T(8,128)})) %all-reduce.7.cloned.1.call-update) | async-done | bytes 3145744 | tf_op jit(solution)/shard_map/psum | solution.py:122
  721.1 2.5 fusion.32
  725.0 2.1 fusion.81
  727.1 4.7 collective-permute-start.11
  731.8 2.1 fusion.85
  733.9 3.5 fusion.68
  (70 shorter events, 10.3 us)
Async XLA Ops:
  6.5 69.9 %copy-start = (bf16[1536,64]{0,1:T(8,128)(2,1)S(1)}, bf16[1536,64]{0,1:T(8,128)(2,1)}, u32[]{:S(2)}) copy-start(bf16[1536,64]{0,1:T(8,128)(2,1)} %param.15) | copy-start | bytes 589828
  45.1 31.1 %copy-start.7 = (bf16[64,1536]{1,0:T(8,128)(2,1)S(1)}, bf16[64,1536]{1,0:T(8,128)(2,1)}, u32[]{:S(2)}) copy-start(bf16[64,1536]{1,0:T(8,128)(2,1)} %param.12) | copy-start | bytes 589828
  45.1 31.1 %copy-start.8 = (bf16[1536,64]{0,1:T(8,128)(2,1)S(1)}, bf16[1536,64]{0,1:T(8,128)(2,1)}, u32[]{:S(2)}) copy-start(bf16[1536,64]{0,1:T(8,128)(2,1)} %param.14) | copy-start | bytes 589828
  45.1 31.1 %copy-start.9 = (s32[64]{0:T(128)S(1)}, s32[64]{0:T(128)}, u32[]{:S(2)}) copy-start(s32[64]{0:T(128)} %param.13) | copy-start | bytes 772
  68.8 33.9 %all-to-all-start = ((f32[16,1,256]{2,1,0:T(1,128)}), f32[16,1,256]{2,1,0:T(1,128)S(1)}, u32[]{:S(2)}, u32[]{:S(2)}) async-start(f32[16,1,256]{2,1,0:T(1,128)} %bitcast.3), calls=%async_computation | async-start | bytes 32768 | tf_op jit(solution)/shard_map/all_to_all | solution.py:88
  102.7 280.5 %all-to-all-start.1 = ((f32[16,256,768]{2,1,0:T(8,128)}), f32[16,256,768]{2,1,0:T(8,128)}, u32[]{:S(2)}, u32[]{:S(2)}) async-start(f32[16,256,768]{2,1,0:T(8,128)} %convert_multiply_fusion), calls=%async_computation.1 | async-start | bytes 25165824 | tf_op jit(solution)/shard_map/all_to_all | solution.py:81
  108.8 396.7 %all-reduce.11.cloned.1.call-start = ((), (), s32[]{:S(2)}) async-start(), calls=%async_computation.4 | async-start | bytes 6291456 | tf_op jit(solution)/shard_map/psum | solution.py:122
  111.8 201.2 %collective-permute-start = (bf16[16,768]{1,0:T(8,128)(2,1)S(1)}, bf16[16,768]{1,0:T(8,128)(2,1)S(1)}, u32[]{:S(2)}, u32[]{:S(2)}) collective-permute-start(bf16[16,768]{1,0:T(8,128)(2,1)S(1)} %get-tuple-element.27), channel_id=1, source_target_pairs={{0,2},{2,4},{4,6},{6,8},{8,10},{10,12},{12,14},{14,16},{16,18},{18... | collective-permute-start | bytes 73736 | tf_op jit(solution)/shard_map/ppermute | solution.py:15
  115.5 199.5 %collective-permute-start.1 = (bf16[16,768]{1,0:T(8,128)(2,1)S(1)}, bf16[16,768]{1,0:T(8,128)(2,1)S(1)}, u32[]{:S(2)}, u32[]{:S(2)}) collective-permute-start(bf16[16,768]{1,0:T(8,128)(2,1)S(1)} %get-tuple-element.26), channel_id=1, source_target_pairs={{2,0},{4,2},{6,4},{8,6},{10,8},{12,10},{14,12},{16,14},{18,16},{20... | collective-permute-start | bytes 73736 | tf_op jit(solution)/shard_map/ppermute | solution.py:18
  415.6 198.0 %all-reduce.9.cloned.1.call-start = ((), (), s32[]{:S(2)}) async-start(), calls=%async_computation.3 | async-start | bytes 6291456 | tf_op jit(solution)/shard_map/psum | solution.py:122
  415.6 10.2 %collective-permute-start.4 = (bf16[8,768]{1,0:T(8,128)(2,1)S(1)}, bf16[8,768]{1,0:T(8,128)(2,1)S(1)}, u32[]{:S(2)}, u32[]{:S(2)}) collective-permute-start(bf16[8,768]{1,0:T(8,128)(2,1)S(1)} %get-tuple-element.23), channel_id=1, source_target_pairs={{0,2},{2,4},{4,6},{6,8},{8,10},{10,12},{12,14},{14,16},{16,18},{18... | collective-permute-start | bytes 36872 | tf_op jit(solution)/shard_map/ppermute | solution.py:15
  421.8 6.2 collective-permute-start.5
  508.0 7.9 %collective-permute-start.2 = (bf16[16,768]{1,0:T(8,128)(2,1)S(1)}, bf16[16,768]{1,0:T(8,128)(2,1)S(1)}, u32[]{:S(2)}, u32[]{:S(2)}) collective-permute-start(bf16[16,768]{1,0:T(8,128)(2,1)S(1)} %get-tuple-element.25), channel_id=1, source_target_pairs={{2,0},{4,2},{6,4},{8,6},{10,8},{12,10},{14,12},{16,14},{18,16},{20... | collective-permute-start | bytes 73736 | tf_op jit(solution)/shard_map/ppermute | solution.py:18
  511.4 6.7 collective-permute-start.3
  520.9 1.2 copy-start.3
  525.4 5.1 copy-start.2
  525.4 195.7 %all-reduce.7.cloned.1.call-start = ((), (), s32[]{:S(2)}) async-start(), calls=%async_computation.2 | async-start | bytes 6291456 | tf_op jit(solution)/shard_map/psum | solution.py:122
  525.5 7.2 collective-permute-start.8
  529.2 5.9 collective-permute-start.9
  616.1 8.3 %collective-permute-start.6 = (bf16[8,768]{1,0:T(8,128)(2,1)S(1)}, bf16[8,768]{1,0:T(8,128)(2,1)S(1)}, u32[]{:S(2)}, u32[]{:S(2)}) collective-permute-start(bf16[8,768]{1,0:T(8,128)(2,1)S(1)} %get-tuple-element.21), channel_id=1, source_target_pairs={{2,0},{4,2},{6,4},{8,6},{10,8},{12,10},{14,12},{16,14},{18,16},{20... | collective-permute-start | bytes 36872 | tf_op jit(solution)/shard_map/ppermute | solution.py:18
  619.4 7.0 copy-start.4
  619.5 7.0 collective-permute-start.7
  629.0 1.2 copy-start.5
  723.7 8.1 %collective-permute-start.10 = (bf16[4,768]{1,0:T(4,128)(2,1)S(1)}, bf16[4,768]{1,0:T(4,128)(2,1)S(1)}, u32[]{:S(2)}, u32[]{:S(2)}) collective-permute-start(bf16[4,768]{1,0:T(4,128)(2,1)S(1)} %get-tuple-element.17), channel_id=1, source_target_pairs={{2,0},{4,2},{6,4},{8,6},{10,8},{12,10},{14,12},{16,14},{18,16},{20... | collective-permute-start | bytes 18440 | tf_op jit(solution)/shard_map/ppermute | solution.py:18
  727.0 6.8 copy-start.6
  727.1 6.8 collective-permute-start.11
  733.9 3.5 copy-start.1
Sparse Core Ops, SparseCore 0:
  415.7 89.7 all-reduce.10
  525.5 87.9 all-reduce.8
  633.6 87.4 all-reduce.6
where the time goes:
time: 749 us; the launch traced here: 744 us
  waiting for transfers between devices  496 us (66%)
  local copies, waits for them, and re-layouts  76.7 us (10%)
  matrix products  55.1 us (7%)
  other arithmetic  53.4 us (7%)
  starting transfers between devices  49.3 us (7%)
  between operations  13.7 us (2%)
    psum x3, waiting for transfers between devices, per_device(): preceding_sum, mid_sum = lax.psum((partial_result, mid_part), 'chan')  237 us
    ppermute x6, waiting for transfers between devices, with_halo(): lax.ppermute(lax.slice_in_dim(block, block.shape[dim] - width, None, axis...  194 us
    all_to_all x1, waiting for transfers between devices, per_device(): lax.all_to_all(contrib.reshape(members, capacity, width_share), ('pos', '...  64.9 us
    scatter-add x1, other arithmetic, per_device(): jax.ops.segment_sum(flat_values, got_place.reshape(-1).astype(jnp.int32),...  29 us
    ppermute x6, starting transfers between devices, with_halo(): lax.ppermute(lax.slice_in_dim(block, block.shape[dim] - width, None, axis...  27.8 us
    dot_general x9, matrix products, per_device(): jnp.dot(act_pad[start:start + local_rows], conv_weight[block_level, kerne...  23.4 us
    gather x1, local copies, waits for them, and re-layouts, per_device(): slot_weight = jnp.where(filled, flat_grad[source], 0.0)  23 us
    gather x1, local copies, waits for them, and re-layouts, per_device(): slot_place = jnp.where(filled, offset[source], 0).astype(jnp.float32)  23 us
  transfers between devices with their start and end apart: 17, of which 5 were waited for; matrix products, arithmetic and copies ran while one was open for 9% of the time, Pallas kernels for 0%

commit v1 on v0

v1 whole, which is shorter than its diff:
```python
import jax
import jax.numpy as jnp
from jax import lax
from jax.sharding import PartitionSpec as P

BASE_DILATION = 4
RANK = 8
SEQ = ("pos", "head")


def gelu_value(value):
    return 0.5 * value * (1.0 + jax.scipy.special.erf(value * 0.7071067811865476))


def gelu_slope(value):
    return (
        0.5 * (1.0 + jax.scipy.special.erf(value * 0.7071067811865476))
        + value * jnp.exp(-0.5 * value * value) * 0.3989422804014327
    )


def from_peer(partial):
    count = lax.axis_size("chan")
    pairs = [(i, (i + 1) % count) for i in range(count)]
    return lax.ppermute(partial.astype(jnp.bfloat16), "chan", pairs).astype(jnp.float32)


def per_device(
    inputs_saved,
    conv_weight,
    expand_weight,
    head_weight,
    batch_of,
    erase_left,
    erase_right,
    bin_gradient,
    cover_bins,
):
    members = lax.axis_size(SEQ)
    place = lax.axis_index(SEQ)
    chan_place = lax.axis_index("chan")
    layers, rows, width = inputs_saved.shape
    taps = conv_weight.shape[1]
    dilation = [BASE_DILATION * 2**n for n in range(layers)]
    reach = [sum(dilation[: n + 1]) for n in range(layers)]
    act_reach = [reach[n] + dilation[n] for n in range(layers)]

    entries = jnp.stack([cover_bins.astype(jnp.float32).T, bin_gradient.astype(jnp.float32).T])
    entries = lax.all_gather(entries, SEQ, axis=2, tiled=True)
    projected = jnp.dot(head_weight, erase_left, preferred_element_type=jnp.float32)
    columns = jnp.arange(erase_left.shape[1]) // RANK
    chosen = (columns[None, :] == batch_of[:, None]).astype(jnp.float32)
    right_share = lax.dynamic_slice_in_dim(erase_right, chan_place * width, width, 0)
    weight_share = lax.dynamic_slice_in_dim(head_weight, chan_place * width, width, 1)
    removed_rows = jnp.dot(
        projected * chosen, right_share.astype(jnp.float32).T, precision=lax.Precision.HIGHEST
    )
    vectors = (weight_share.astype(jnp.float32) - removed_rows).astype(jnp.bfloat16)
    vectors = lax.all_gather(vectors, SEQ, axis=0, tiled=True)

    forward = [(i, i + 1) for i in range(members - 1)]
    backward = [(b, a) for a, b in forward]
    low = lax.ppermute(
        jnp.concatenate([inputs_saved[n, rows - act_reach[n] :] for n in range(layers)]), SEQ, forward
    )
    high = lax.ppermute(
        jnp.concatenate([inputs_saved[n, : act_reach[n]] for n in range(layers)]), SEQ, backward
    )
    around, slopes = [], []
    start = 0
    for n in range(layers):
        stop = start + act_reach[n]
        around.append(jnp.concatenate([low[start:stop], inputs_saved[n], high[start:stop]]))
        start = stop

    for n in range(layers):
        size = rows + 2 * reach[n]
        act = gelu_value(around[n].astype(jnp.float32)).astype(jnp.bfloat16)
        wide = jnp.concatenate(
            [act[t * dilation[n] : t * dilation[n] + size] for t in range(taps)], axis=1
        )
        weight = conv_weight[n].reshape(taps * width, conv_weight.shape[3])
        part = jnp.dot(wide, weight, preferred_element_type=jnp.float32)
        position = place * rows - reach[n] + jnp.arange(size)
        inside = (position >= 0) & (position < members * rows)
        slopes.append((part, inside))

    top = layers - 1
    position = (place * rows - reach[top] + jnp.arange(rows + 2 * reach[top])).astype(jnp.float32)
    spread = jnp.sum(
        jnp.where(entries[0][:, None, :] == position[None, :, None], entries[1][:, None, :], 0.0),
        axis=0,
    ).astype(jnp.bfloat16)
    grad = jnp.dot(spread, vectors, preferred_element_type=jnp.float32)

    peers = [None] * layers
    for n in reversed(range(layers)):
        peers[n] = from_peer(slopes[n][0])

    for n in reversed(range(layers)):
        size = rows + 2 * (reach[n] - dilation[n])
        mid_part = lax.dot_general(
            grad.astype(jnp.bfloat16),
            expand_weight[n],
            (((1,), (1,)), ((), ())),
            preferred_element_type=jnp.float32,
        )
        part, inside = slopes[n]
        slope = jnp.where(inside[:, None], gelu_slope(part + peers[n]), 0.0)
        grad_pre = ((mid_part + from_peer(mid_part)) * slope).astype(jnp.bfloat16)
        grad_act = jnp.zeros((size, width), jnp.float32)
        for t in range(taps):
            first = (taps - 1 - t) * dilation[n]
            grad_act = grad_act + lax.dot_general(
                grad_pre[first : first + size],
                conv_weight[n, t],
                (((1,), (1,)), ((), ())),
                preferred_element_type=jnp.float32,
            )
        saved = around[n][2 * dilation[n] : 2 * dilation[n] + size].astype(jnp.float32)
        grad = grad[dilation[n] : dilation[n] + size] + grad_act * gelu_slope(saved)
    return grad.astype(jnp.bfloat16)


def solution(mesh):
    return jax.shard_map(
        per_device,
        mesh=mesh,
        in_specs=(
            P(None, ("pos", "head"), "chan"),
            P(None, None, "chan", None),
            P(None, None, "chan"),
            P(("pos", "head"), None),
            P(("pos", "head")),
            P(),
            P(),
            P(("pos", "head"), None),
            P(("pos", "head"), None),
        ),
        out_specs=P(("pos", "head"), "chan"),
        check_vma=False,
    )
```

time: 749 us -> 224 us (0.30)
  waiting for transfers between devices: 496 us -> 73.7 us
  local copies, waits for them, and re-layouts: 76.7 us -> 18.7 us
  blocking collectives: 0 us -> 48.6 us
  starting transfers between devices: 49.3 us -> 15.7 us
  other arithmetic: 53.4 us -> 20.1 us
  matrix products: 55.1 us -> 32.5 us
    psum x3 -> x0, waiting for transfers between devices: 237 us -> none  [per_device(): preceding_sum, mid_sum = lax.psum((partial_result, mid_part), 'chan')]
    ppermute x12 -> x8, waiting for transfers between devices: 194 us -> 73.7 us  [the longest x6 73.7 us: from_peer(): lax.ppermute(partial.astype(jnp.bfloat16), 'chan', pairs)]
    all_to_all x2 -> x0, waiting for transfers between devices: 64.9 us -> none  [the longest x1 64.9 us: per_device(): lax.all_to_all(contrib.reshape(members, capacity, width_share), ('pos', '...]
    gather x3 -> x0, local copies, waits for them, and re-layouts: 63.8 us -> none  [the longest x1 23 us: per_device(): slot_weight = jnp.where(filled, flat_grad[source], 0.0)]
    all_gather x0 -> x1, blocking collectives: none -> 48.6 us  [per_device(): entries = lax.all_gather(entries, SEQ, axis=2, tiled=True)]
    scatter-add x1 -> x0, other arithmetic: 29 us -> none  [per_device(): jax.ops.segment_sum(flat_values, got_place.reshape(-1).astype(jnp.int32),...]
    dot_general x21 -> x16, matrix products: 54.7 us -> 29.5 us  [the longest x9 14.1 us: per_device(): lax.dot_general(grad_pre[first:first + size], conv_weight[n, t], (((1,),...]
    ppermute x12 -> x8, starting transfers between devices: 35.8 us -> 15.7 us  [the longest x6 8.86 us: from_peer(): lax.ppermute(partial.astype(jnp.bfloat16), 'chan', pairs)]
  transfers between devices with their start and end apart: 17 -> 9, of which waited for: 5 -> 6; matrix products, arithmetic and copies ran while one was open for 9% -> 25% of each run, Pallas kernels for 0% -> 0%
where the time goes in v1:
time: 224 us; the launch traced here: 223 us
  waiting for transfers between devices  73.7 us (33%)
  blocking collectives  48.6 us (22%)
  matrix products  32.5 us (15%)
  other arithmetic  20.1 us (9%)
  local copies, waits for them, and re-layouts  18.7 us (8%)
  starting transfers between devices  15.7 us (7%)
  between operations  13.8 us (6%)
    ppermute x6, waiting for transfers between devices, from_peer(): lax.ppermute(partial.astype(jnp.bfloat16), 'chan', pairs)  73.7 us
    all_gather x1, blocking collectives, per_device(): entries = lax.all_gather(entries, SEQ, axis=2, tiled=True)  48.6 us
    dot_general x9, matrix products, per_device(): lax.dot_general(grad_pre[first:first + size], conv_weight[n, t], (((1,),...  14.1 us
    reduce_sum x1, other arithmetic, per_device(): jnp.sum(jnp.where(entries[0][:, None, :] == position[None, :, None], entr...  10.7 us
    dot_general x3, matrix products, per_device(): part = jnp.dot(wide, weight, preferred_element_type=jnp.float32)  8.91 us
    ppermute x6, starting transfers between devices, from_peer(): lax.ppermute(partial.astype(jnp.bfloat16), 'chan', pairs)  8.86 us
    slice x1, local copies, waits for them, and re-layouts, per_device(): weight = conv_weight[n].reshape(taps * width, conv_weight.shape[3])  7.28 us
    convert_element_type x3, other arithmetic, per_device(): grad_pre = ((mid_part + from_peer(mid_part)) * slope).astype(jnp.bfloat16)  6.3 us
  transfers between devices with their start and end apart: 9, of which 6 were waited for; matrix products, arithmetic and copies ran while one was open for 25% of the time, Pallas kernels for 0%

profile of v1, /device:TPU:0, one launch (start us, length us, event | category | flops | bytes accessed | tf_op | source)
XLA Modules:
  0.0 223.2 jit_solution(1462261014274174122)
XLA Ops:
  6.5 1.0 slice_bitcast_fusion.4
  7.5 0.8 slice_bitcast_fusion.6
  8.3 0.7 slice_bitcast_fusion.8
  9.1 1.3 collective-permute-start.2
  10.4 0.7 pad_maximum_fusion.2
  11.1 5.5 %collective-permute-start.1 = (bf16[72,768]{1,0:T(8,128)(2,1)}, bf16[72,768]{1,0:T(8,128)(2,1)S(1)}, u32[]{:S(2)}, u32[]{:S(2)}) collective-permute-start(bf16[72,768]{1,0:T(8,128)(2,1)} %pad_maximum_fusion.2), channel_id=1, source_target_pairs={{0,2},{2,4},{4,6},{6,8},{8,10},{10,12},{12,14},{14,16},{16,18},{18... | collective-permute-start | bytes 331784 | tf_op jit(solution)/shard_map/ppermute | solution.py:63
  16.6 1.2 convolution_select_fusion
  17.9 1.8 fusion.113
  19.7 1.8 slice_bitcast_fusion.1
  21.5 7.3 %fusion.149 = (bf16[1,3,768,768]{3,2,1,0:T(8,128)(2,1)}, bf16[1,3,768,768]{3,2,1,0:T(8,128)(2,1)}, bf16[1,3,768,768]{3,2,1,0:T(8,128)(2,1)}) fusion(bf16[3,3,768,768]{3,2,1,0:T(8,128)(2,1)} %param.10), kind=kLoop, calls=%fused_computation.188 | loop fusion | bytes 21233664 | tf_op jit(solution)/shard_map/slice | solution.py:82
  28.9 48.6 %all_gather.6 = f32[2,32,1024]{1,0,2:T(2,128)S(1)} all-gather(f32[2,32,64]{1,0,2:T(2,128)S(1)} %copy.18), channel_id=1, replica_groups=mesh['pos'=4,'head'=4,'chan'=2] {'pos','head'}, dimensions={2}, use_global_device_ids=true | all-gather | bytes 278528 | tf_op jit(solution)/shard_map/all_gather | solution.py:49
  77.5 1.6 fusion.150
  79.1 1.2 copy.20
  80.5 10.7 %select_reduce_fusion = bf16[568,1024]{1,0:T(8,128)(2,1)} fusion(f32[32,1024]{1,0:T(8,128)S(1)} %copy.20, f32[32,1024]{1,0:T(8,128)S(1)} %copy.19, f32[568]{0:T(1024)S(1)} %fusion.141), kind=kLoop, calls=%fused_computation | loop fusion | flops 55255040 | bytes 1427680 | tf_op jit(solution)/shard_map/reduce_sum | solution.py:90
  91.3 0.6 copy-done.10
  92.6 1.8 copy-done.5
  94.5 3.8 %fusion.155 = (bf16[568,768]{1,0:T(8,128)(2,1)}, f32[568,768]{1,0:T(8,128)}) fusion(bf16[2304,768]{1,0:T(8,128)(2,1)S(1)} %bitcast.91, bf16[568,768]{1,0:T(8,128)(2,1)S(1)} %get-tuple-element.24, bf16[568,768]{1,0:T(8,128)(2,1)S(1)} %get-tuple-element.25, bf16[568,768]{1,0:T(8,128)(2,1)S(1)} %get-tuple-element.23), kind=kOutput, calls=%fused_computation.194 | convolution fusion | flops 2018408448 | bytes 8773632 | tf_op jit(solution)/shard_map/dot_general | solution.py:83
  98.3 1.9 collective-permute-start.3
  100.1 1.4 fusion.30
  101.6 3.0 %fusion.160 = f32[568,768]{1,0:T(8,128)S(1)} fusion(bf16[568,1024]{1,0:T(8,128)(2,1)} %select_reduce_fusion, bf16[1024,768]{1,0:T(8,128)(2,1)} %all-gather.2.cloned.1.call-done), kind=kOutput, calls=%fused_computation.199 | convolution fusion | flops 893386752 | bytes 4481024 | tf_op jit(solution)/shard_map/dot_general | solution.py:94
  104.6 0.9 fusion.156
  105.9 0.7 copy-done.4
  106.6 2.1 fusion.157
  108.7 1.3 collective-permute-start.5
  110.4 10.5 %collective-permute-done.3 = bf16[568,768]{1,0:T(8,128)(2,1)} collective-permute-done((bf16[568,768]{1,0:T(8,128)(2,1)}, bf16[568,768]{1,0:T(8,128)(2,1)}, u32[]{:S(2)}, u32[]{:S(2)}) %collective-permute-start.3) | collective-permute-done | bytes 872480 | tf_op jit(solution)/shard_map/ppermute | solution.py:25
  120.9 18.6 %collective-permute-done = bf16[568,768]{1,0:T(8,128)(2,1)S(1)} collective-permute-done((bf16[568,768]{1,0:T(8,128)(2,1)S(1)}, bf16[568,768]{1,0:T(8,128)(2,1)S(1)}, u32[]{:S(2)}, u32[]{:S(2)}) %collective-permute-start) | collective-permute-done | bytes 872480 | tf_op jit(solution)/shard_map/ppermute | solution.py:25
  139.5 2.6 %fusion.28 = bf16[568,768]{1,0:T(8,128)(2,1)S(1)} fusion(f32[568,768]{1,0:T(8,128)S(1)} %copy-done.6, bf16[568,768]{1,0:T(8,128)(2,1)} %collective-permute-done.3, f32[568,768]{1,0:T(8,128)S(1)} %get-tuple-element.37, bf16[568,768]{1,0:T(8,128)(2,1)S(1)} %collective-permute-done, pred[568]{0:T(1024)(128)(4,1)S(1)} %fusion.142), kind=kLoop, calls=%fused_computation.50 | loop fusion | flops 6543360 | bytes 6107704 | tf_op jit(solution)/shard_map/convert_element_type | solution.py:110
  142.1 0.8 fusion.95
  143.0 0.9 fusion.93
  143.9 1.3 fusion.47
  145.2 0.9 fusion.158
  146.1 1.9 collective-permute-start.4
  148.3 3.0 %fusion.154 = (bf16[520,768]{1,0:T(8,128)(2,1)}, f32[520,768]{1,0:T(8,128)S(1)}) fusion(bf16[2304,768]{1,0:T(8,128)(2,1)S(1)} %bitcast.89, bf16[520,768]{1,0:T(8,128)(2,1)S(1)} %get-tuple-element.30, bf16[520,768]{1,0:T(8,128)(2,1)S(1)} %get-tuple-element.31, bf16[520,768]{1,0:T(8,128)(2,1)S(1)} %get-tuple-element.29), kind=kOutput, calls=%fused_computation.193 | convolution fusion | flops 1847838720 | bytes 8331264 | tf_op jit(solution)/shard_map/dot_general | solution.py:83
  151.2 1.7 collective-permute-start.7
  152.9 4.2 %collective-permute-done.5 = bf16[536,768]{1,0:T(8,128)(2,1)S(1)} collective-permute-done((bf16[536,768]{1,0:T(8,128)(2,1)S(1)}, bf16[536,768]{1,0:T(8,128)(2,1)S(1)}, u32[]{:S(2)}, u32[]{:S(2)}) %collective-permute-start.5) | collective-permute-done | bytes 823328 | tf_op jit(solution)/shard_map/ppermute | solution.py:25
  157.1 17.6 %collective-permute-done.4 = bf16[536,768]{1,0:T(8,128)(2,1)S(1)} collective-permute-done((bf16[536,768]{1,0:T(8,128)(2,1)S(1)}, bf16[536,768]{1,0:T(8,128)(2,1)S(1)}, u32[]{:S(2)}, u32[]{:S(2)}) %collective-permute-start.4) | collective-permute-done | bytes 823328 | tf_op jit(solution)/shard_map/ppermute | solution.py:25
  174.8 1.3 fusion.39
  176.1 0.8 fusion.87
  176.9 0.8 fusion.85
  178.1 1.3 fusion.66
  179.4 1.8 fusion.159
  181.2 1.9 collective-permute-start.6
  183.1 8.9 %collective-permute-done.7 = bf16[520,768]{1,0:T(8,128)(2,1)} collective-permute-done((bf16[520,768]{1,0:T(8,128)(2,1)}, bf16[520,768]{1,0:T(8,128)(2,1)}, u32[]{:S(2)}, u32[]{:S(2)}) %collective-permute-start.7) | collective-permute-done | bytes 798752 | tf_op jit(solution)/shard_map/ppermute | solution.py:25
  192.0 13.8 %collective-permute-done.6 = bf16[520,768]{1,0:T(8,128)(2,1)} collective-permute-done((bf16[520,768]{1,0:T(8,128)(2,1)}, bf16[520,768]{1,0:T(8,128)(2,1)}, u32[]{:S(2)}, u32[]{:S(2)}) %collective-permute-start.6) | collective-permute-done | bytes 798752 | tf_op jit(solution)/shard_map/ppermute | solution.py:25
  205.8 2.4 %fusion.58 = bf16[520,768]{1,0:T(8,128)(2,1)S(1)} fusion(f32[520,768]{1,0:T(8,128)S(1)} %get-tuple-element.33, bf16[520,768]{1,0:T(8,128)(2,1)} %collective-permute-done.7, f32[520,768]{1,0:T(8,128)S(1)} %get-tuple-element.43, bf16[520,768]{1,0:T(8,128)(2,1)} %collective-permute-done.6, pred[520]{0:T(1024)(128)(4,1)S(1)} %fusion.144), kind=kLoop, calls=%fused_computation.80 | loop fusion | flops 5990400 | bytes 5591560 | tf_op jit(solution)/shard_map/convert_element_type | solution.py:110
  208.2 2.1 fusion.79
  210.3 2.2 fusion.77
  212.6 3.7 %fusion.75 = bf16[512,768]{1,0:T(8,128)(2,1)} fusion(f32[512,768]{1,0:T(8,128)S(1)} %fusion.79, f32[512,768]{1,0:T(8,128)S(1)} %fusion.77, f32[520,768]{1,0:T(8,128)S(1)} %copy-done.8, bf16[3,3,768,768]{3,2,1,0:T(8,128)(2,1)} %param.10, bf16[520,768]{1,0:T(8,128)(2,1)S(1)} %fusion.58, bf16[3,512,768]{2,1,0:T(8,128)(2,1)} %param.9), kind=kOutput, calls=%fused_computation.97 | convolution fusion | flops 609484800 | bytes 8257536 | tf_op jit(solution)/shard_map/dot_general | solution.py:114
  (64 shorter events, 2.5 us)
Async XLA Ops:
  6.5 11.3 %copy-start = (bf16[1536,64]{0,1:T(8,128)(2,1)S(1)}, bf16[1536,64]{0,1:T(8,128)(2,1)}, u32[]{:S(2)}) copy-start(bf16[1536,64]{0,1:T(8,128)(2,1)} %param.15) | copy-start | bytes 589828
  6.5 95.0 %all-gather.2.cloned.1.call-start = ((), (), s32[]{:S(2)}) async-start(), calls=%async_computation | async-start | bytes 1671168 | tf_op jit(solution)/shard_map/all_gather | solution.py:59
  9.1 82.1 %collective-permute-start.2 = (bf16[72,768]{1,0:T(8,128)(2,1)S(1)}, bf16[72,768]{1,0:T(8,128)(2,1)S(1)}, u32[]{:S(2)}, u32[]{:S(2)}) collective-permute-start(bf16[72,768]{1,0:T(8,128)(2,1)S(1)} %pad_maximum_fusion.3), channel_id=1, source_target_pairs={{2,0},{4,2},{6,4},{8,6},{10,8},{12,10},{14,12},{16,14},{18,16},{20... | collective-permute-start | bytes 331784 | tf_op jit(solution)/shard_map/ppermute | solution.py:66
  11.1 80.2 %collective-permute-start.1 = (bf16[72,768]{1,0:T(8,128)(2,1)}, bf16[72,768]{1,0:T(8,128)(2,1)S(1)}, u32[]{:S(2)}, u32[]{:S(2)}) collective-permute-start(bf16[72,768]{1,0:T(8,128)(2,1)} %pad_maximum_fusion.2), channel_id=1, source_target_pairs={{0,2},{2,4},{4,6},{6,8},{8,10},{10,12},{12,14},{14,16},{16,18},{18... | collective-permute-start | bytes 331784 | tf_op jit(solution)/shard_map/ppermute | solution.py:63
  21.5 7.3 %copy-start.13 = (bf16[64,32]{0,1:T(8,128)(2,1)S(1)}, bf16[64,32]{0,1:T(8,128)(2,1)}, u32[]{:S(2)}) copy-start(bf16[64,32]{0,1:T(8,128)(2,1)} %param.16) | copy-start | bytes 12292
  21.5 7.3 %copy-start.12 = (s32[64,32]{0,1:T(8,128)S(1)}, s32[64,32]{0,1:T(8,128)}, u32[]{:S(2)}) copy-start(s32[64,32]{0,1:T(8,128)} %param.17) | copy-start | bytes 24580
  91.2 0.6 copy-start.10
  91.2 0.7 copy-start.11
  92.4 2.0 copy-start.5
  94.4 5.7 %slice-start.3 = ((bf16[72,768]{1,0:T(8,128)(2,1)}), bf16[20,768]{1,0:T(8,128)(2,1)S(1)}, s32[]{:S(2)}) async-start(bf16[72,768]{1,0:T(8,128)(2,1)} %copy-done.10), calls=%async_computation.4 | async-start | bytes 73728 | tf_op jit(solution)/shard_map/slice | solution.py:73
  94.5 5.7 %slice-start.5 = ((bf16[72,768]{1,0:T(8,128)(2,1)}), bf16[20,768]{1,0:T(8,128)(2,1)S(1)}, s32[]{:S(2)}) async-start(bf16[72,768]{1,0:T(8,128)(2,1)} %copy-done.11), calls=%async_computation.6 | async-start | bytes 73728 | tf_op jit(solution)/shard_map/slice | solution.py:73
  98.3 22.6 %collective-permute-start.3 = (bf16[568,768]{1,0:T(8,128)(2,1)}, bf16[568,768]{1,0:T(8,128)(2,1)}, u32[]{:S(2)}, u32[]{:S(2)}) collective-permute-start(bf16[568,768]{1,0:T(8,128)(2,1)} %get-tuple-element.34), channel_id=1, source_target_pairs={{0,1},{1,0},{2,3},{3,2},{4,5},{5,4},{6,7},{7,6},{8,9},{9,8},{10,11... | collective-permute-start | bytes 2617352 | tf_op jit(solution)/shard_map/ppermute | solution.py:25
  101.6 3.0 %copy-start.2 = (bf16[3,768,768]{2,1,0:T(8,128)(2,1)S(1)}, bf16[3,768,768]{2,1,0:T(8,128)(2,1)}, u32[]{:S(2)}) copy-start(bf16[3,768,768]{2,1,0:T(8,128)(2,1)} %param.11) | copy-start | bytes 10616836
  104.6 2.0 copy-start.4
  105.5 34.0 %collective-permute-start = (bf16[568,768]{1,0:T(8,128)(2,1)S(1)}, bf16[568,768]{1,0:T(8,128)(2,1)S(1)}, u32[]{:S(2)}, u32[]{:S(2)}) collective-permute-start(bf16[568,768]{1,0:T(8,128)(2,1)S(1)} %get-tuple-element.36), channel_id=1, source_target_pairs={{0,1},{1,0},{2,3},{3,2},{4,5},{5,4},{6,7},{7,6},{8,9},{9,8},{10,11... | collective-permute-start | bytes 2617352 | tf_op jit(solution)/shard_map/ppermute | solution.py:25
  105.7 36.4 %slice-start = ((s8[10616832]{0:T(1024)(128)(4,1)}), s8[4194304]{0:T(1024)(128)(4,1)S(1)}, s32[]{:S(2)}) async-start(s8[10616832]{0:T(1024)(128)(4,1)} %bitcast.87), calls=%async_computation.1 | async-start | bytes 8388608
  106.6 3.5 %slice-start.4 = ((bf16[72,768]{1,0:T(8,128)(2,1)}), bf16[8,768]{1,0:T(8,128)(2,1)S(1)}, s32[]{:S(2)}) async-start(bf16[72,768]{1,0:T(8,128)(2,1)} %copy-done.10), calls=%async_computation.5 | async-start | bytes 24576 | tf_op jit(solution)/shard_map/slice | solution.py:73
  106.6 3.5 %slice-start.6 = ((bf16[72,768]{1,0:T(8,128)(2,1)}), bf16[8,768]{1,0:T(8,128)(2,1)S(1)}, s32[]{:S(2)}) async-start(bf16[72,768]{1,0:T(8,128)(2,1)} %copy-done.11), calls=%async_computation.7 | async-start | bytes 24576 | tf_op jit(solution)/shard_map/slice | solution.py:73
  106.6 32.9 %copy-start.6 = (f32[568,768]{1,0:T(8,128)S(1)}, f32[568,768]{1,0:T(8,128)}, u32[]{:S(2)}) copy-start(f32[568,768]{1,0:T(8,128)} %get-tuple-element.35) | copy-start | bytes 5234692
  106.6 35.5 %slice-start.1 = ((s8[10616832]{0:T(1024)(128)(4,1)}), s8[4194304]{0:T(1024)(128)(4,1)S(1)}, s32[]{:S(2)}) async-start(s8[10616832]{0:T(1024)(128)(4,1)} %bitcast.87), calls=%async_computation.2 | async-start | bytes 8388608
  106.6 35.5 %slice-start.2 = ((s8[10616832]{0:T(1024)(128)(4,1)}), s8[2228224]{0:T(1024)(128)(4,1)S(1)}, s32[]{:S(2)}) async-start(s8[10616832]{0:T(1024)(128)(4,1)} %bitcast.87), calls=%async_computation.3 | async-start | bytes 4456448
  108.7 48.4 %collective-permute-start.5 = (bf16[536,768]{1,0:T(8,128)(2,1)S(1)}, bf16[536,768]{1,0:T(8,128)(2,1)S(1)}, u32[]{:S(2)}, u32[]{:S(2)}) collective-permute-start(bf16[536,768]{1,0:T(8,128)(2,1)S(1)} %get-tuple-element.38), channel_id=1, source_target_pairs={{0,1},{1,0},{2,3},{3,2},{4,5},{5,4},{6,7},{7,6},{8,9},{9,8},{10,11... | collective-permute-start | bytes 2469896 | tf_op jit(solution)/shard_map/ppermute | solution.py:25
  146.1 2.2 copy-start.3
  146.1 28.7 %collective-permute-start.4 = (bf16[536,768]{1,0:T(8,128)(2,1)S(1)}, bf16[536,768]{1,0:T(8,128)(2,1)S(1)}, u32[]{:S(2)}, u32[]{:S(2)}) collective-permute-start(bf16[536,768]{1,0:T(8,128)(2,1)S(1)} %get-tuple-element.40), channel_id=1, source_target_pairs={{0,1},{1,0},{2,3},{3,2},{4,5},{5,4},{6,7},{7,6},{8,9},{9,8},{10,11... | collective-permute-start | bytes 2469896 | tf_op jit(solution)/shard_map/ppermute | solution.py:25
  151.2 40.8 %collective-permute-start.7 = (bf16[520,768]{1,0:T(8,128)(2,1)}, bf16[520,768]{1,0:T(8,128)(2,1)}, u32[]{:S(2)}, u32[]{:S(2)}) collective-permute-start(bf16[520,768]{1,0:T(8,128)(2,1)} %get-tuple-element.32), channel_id=1, source_target_pairs={{0,1},{1,0},{2,3},{3,2},{4,5},{5,4},{6,7},{7,6},{8,9},{9,8},{10,11... | collective-permute-start | bytes 2396168 | tf_op jit(solution)/shard_map/ppermute | solution.py:25
  176.9 1.2 copy-start.9
  179.4 1.8 copy-start.7
  181.2 24.6 %collective-permute-start.6 = (bf16[520,768]{1,0:T(8,128)(2,1)}, bf16[520,768]{1,0:T(8,128)(2,1)}, u32[]{:S(2)}, u32[]{:S(2)}) collective-permute-start(bf16[520,768]{1,0:T(8,128)(2,1)} %get-tuple-element.42), channel_id=1, source_target_pairs={{0,1},{1,0},{2,3},{3,2},{4,5},{5,4},{6,7},{7,6},{8,9},{9,8},{10,11... | collective-permute-start | bytes 2396168 | tf_op jit(solution)/shard_map/ppermute | solution.py:25
  210.3 2.2 %copy-start.8 = (f32[520,768]{1,0:T(8,128)S(1)}, f32[520,768]{1,0:T(8,128)}, u32[]{:S(2)}) copy-start(f32[520,768]{1,0:T(8,128)} %copy-done.7) | copy-start | bytes 4792324
  212.6 3.7 %copy-start.1 = (bf16[1536,64]{0,1:T(8,128)(2,1)S(1)}, bf16[1536,64]{0,1:T(8,128)(2,1)}, u32[]{:S(2)}) copy-start(bf16[1536,64]{0,1:T(8,128)(2,1)} %param.15) | copy-start | bytes 589828
Sparse Core Ops, SparseCore 0:
  19.8 44.7 all-gather.1

commit v2 on v1

v2 whole, which is shorter than its diff:
```python
import functools

import jax
import jax.numpy as jnp
from jax import lax
from jax.experimental import pallas as pl
from jax.experimental.pallas import tpu as pltpu
from jax.sharding import PartitionSpec as P

BASE_DILATION = 4
RANK = 8
SEQ = ("pos", "head")
MESH = pl.DeviceIdType.MESH
BF = jnp.bfloat16
F32 = jnp.float32
TILE = 256
STEP = 16
NT = (((1,), (1,)), ((), ()))


def gelu_value(value):
    return 0.5 * value * (1.0 + lax.erf(value * 0.7071067811865476))


def gelu_slope(value):
    return (
        0.5 * (1.0 + lax.erf(value * 0.7071067811865476))
        + value * jnp.exp(-0.5 * value * value) * 0.3989422804014327
    )


def up(value, unit):
    return -(-value // unit) * unit


def frames(layers):
    wide, out, saved, before = [], [], [], 0
    for n in range(layers):
        dilation = BASE_DILATION * 2**n
        out.append(before)
        before = up(before + dilation, 8)
        wide.append(before)
        saved.append(up(before + dilation, 16))
    return wide, out, saved


def kernel(
    layers, rows, width, inner, taps, npos, nhead, exps,
    inputs_ref, conv_ref, expand_ref, pay_ref,
    out_ref,
    sv0, sv1, sv2, conv, expand, vall, sbuf, actf, aw, pp, ps, pr, mp, ms, mr,
    sp, ss, ga, gb, acc, gradbf, gpf, gpw,
    load_sem, own_sem, halo_s, halo_r, s1, r1, s2p, r2p, s2x, r2x, s3, r3, ps_s, ps_r, ms_s, ms_r,
):
    sv = [sv0, sv1, sv2]
    wide, outs, saved = frames(layers)
    dil = [BASE_DILATION * 2**n for n in range(layers)]
    members = npos * nhead
    p, h = lax.axis_index("pos"), lax.axis_index("head")
    peer = {"chan": 1 - lax.axis_index("chan")}
    place = p * nhead + h
    after = lax.rem(place + 1, members)
    ahead = lax.rem(place + members - 1, members)
    follow = {"pos": after // nhead, "head": lax.rem(after, nhead)}
    precede = {"pos": ahead // nhead, "head": lax.rem(ahead, nhead)}
    mate = p + 1 - 2 * lax.rem(p, 2)
    partner = {"pos": mate}
    nx = npos // 2
    ct_n, jt_n = width // TILE, inner // TILE

    def remote(src, dst, send, recv, device):
        return pltpu.make_async_remote_copy(
            src_ref=src, dst_ref=dst, send_sem=send, recv_sem=recv, device_id=device, device_id_type=MESH
        )

    def head_of(dh):
        return lax.rem(h + nhead - dh, nhead)

    def pos_of(start, dx):
        return lax.rem(start + npos - 2 * dx, npos)

    loads = {}
    at = 0
    for n in reversed(range(layers)):
        loads["saved", n] = pltpu.make_async_copy(
            inputs_ref.at[n], sv[n].at[pl.ds(saved[n], rows)], load_sem.at[at]
        )
        loads["conv", n] = pltpu.make_async_copy(conv_ref.at[n], conv.at[n], load_sem.at[at + 1])
        loads["expand", n] = pltpu.make_async_copy(expand_ref.at[n], expand.at[n], load_sem.at[at + 2])
        at += 3
    own = pltpu.make_async_copy(pay_ref, vall.at[p, h], own_sem)
    own.start()
    loads["saved", layers - 1].start()
    loads["conv", layers - 1].start()

    barrier = pltpu.get_barrier_semaphore()
    known = [follow, precede, peer, partner]
    known += [{"head": lax.rem(h + dh, nhead)} for dh in range(1, nhead)]
    known += [{"pos": lax.rem(p + 2 * dx, npos)} for dx in range(1, nx)]
    for device in known:
        pl.semaphore_signal(barrier, inc=1, device_id=device, device_id_type=MESH)
    pl.semaphore_wait(barrier, len(known))

    halos = {}
    for n in reversed(range(layers)):
        k = saved[n]
        halos[n] = [
            remote(inputs_ref.at[n, pl.ds(rows - k, k)], sv[n].at[pl.ds(0, k)],
                   halo_s.at[n, 0], halo_r.at[n, 0], follow),
            remote(inputs_ref.at[n, pl.ds(0, k)], sv[n].at[pl.ds(rows + k, k)],
                   halo_s.at[n, 1], halo_r.at[n, 1], precede),
        ]
    for copy in halos[layers - 1]:
        copy.start()
    first = [
        remote(pay_ref, vall.at[p, h], s1.at[dh], r1.at[dh], {"head": lax.rem(h + dh, nhead)})
        for dh in range(1, nhead)
    ]
    for copy in first:
        copy.start()
    for n in reversed(range(layers - 1)):
        for copy in halos[n]:
            copy.start()
    for n in reversed(range(layers)):
        if n < layers - 1:
            loads["saved", n].start()
            loads["conv", n].start()
        loads["expand", n].start()

    def inside(start, count):
        spot = place * rows + start + lax.broadcasted_iota(jnp.int32, (count, TILE), 0)
        return (spot >= 0) & (spot < members * rows)

    def make_pre(n, push):
        size = rows + 2 * wide[n]
        loads["saved", n].wait()
        for copy in halos[n]:
            copy.wait()

        def activate(r, _):
            place_at = pl.ds(pl.multiple_of(r * STEP, STEP), STEP)
            keep = inside(r * STEP - saved[n], STEP)
            for ct in range(ct_n):
                value = sv[n][place_at, ct * TILE : (ct + 1) * TILE].astype(F32)
                actf[ct, place_at, :] = jnp.where(keep, gelu_value(value), 0.0)
            return 0

        lax.fori_loop(0, (rows + 2 * saved[n]) // STEP, activate, 0)
        for t in range(taps):
            begin = saved[n] - wide[n] + (t - 1) * dil[n]
            for ct in range(ct_n):
                aw[t * ct_n + ct, 0:size, :] = actf[ct, begin : begin + size, :].astype(BF)
        loads["conv", n].wait()

        def column(jt, _):
            cols = pl.ds(pl.multiple_of(jt * TILE, TILE), TILE)
            total = None
            for t in range(taps):
                for ct in range(ct_n):
                    term = jnp.dot(
                        aw[t * ct_n + ct, 0:size, :],
                        conv[n, t, ct * TILE : (ct + 1) * TILE, cols],
                        preferred_element_type=F32,
                    )
                    total = term if total is None else total + term
            pp[n, jt, 0:size, :] = total
            ps[n, jt, 0:size, :] = total.astype(BF)
            if push:
                pre_copy(n, jt).start()
            return 0

        lax.fori_loop(0, jt_n, column, 0)

    def pre_copy(n, jt):
        size = rows + 2 * wide[n]
        return remote(ps.at[n, jt, pl.ds(0, size)], pr.at[n, jt, pl.ds(0, size)],
                      ps_s.at[n, jt], ps_r.at[n, jt], peer)

    def mid_copy(n, jt):
        size = rows + 2 * wide[n]
        return remote(ms.at[n, jt, pl.ds(0, size)], mr.at[n, jt, pl.ds(0, size)],
                      ms_s.at[n, jt], ms_r.at[n, jt], peer)

    top = layers - 1
    make_pre(top, True)

    own.wait()
    to_mate, to_x = [], []
    for dh in range(nhead):
        if dh:
            first[dh - 1].wait()
        block = vall.at[p, head_of(dh)]
        for dx in range(1, nx):
            copy = remote(block, block, s2x.at[dx, dh], r2x.at[dx, dh], {"pos": lax.rem(p + 2 * dx, npos)})
            copy.start()
            to_x.append((dx, dh, copy))
        copy = remote(block, block, s2p.at[dh], r2p.at[dh], partner)
        copy.start()
        to_mate.append(copy)

    if layers > 1:
        make_pre(top - 1, True)

    size_top = rows + 2 * wide[top]

    def clear(r, _):
        at_rows = pl.ds(pl.multiple_of(r * STEP, STEP), STEP)
        for ct in range(ct_n):
            ga[ct, at_rows, :] = jnp.zeros((STEP, TILE), F32)
        return 0

    lax.fori_loop(0, size_top // STEP, clear, 0)
    lanes = 2 * exps
    part_rows = size_top // 3

    def add_slab(slab):
        def pair(i, _):
            values = []
            for side in range(2):
                a = 2 * i + side
                words = vall[slab, a, :, width : width + lanes].astype(F32)
                spots = words[0:16] * 256.0 + words[16:32]
                heights = words[32:48]
                for rt in range(3):
                    line = (place * rows - wide[top] + rt * part_rows).astype(F32)
                    row = line + lax.broadcasted_iota(jnp.int32, (part_rows, lanes), 0).astype(F32)
                    found = jnp.zeros((part_rows, lanes), F32)
                    for k in range(16):
                        found = found + jnp.where(spots[k : k + 1] == row, heights[k : k + 1], 0.0)
                    sbuf[rt * part_rows : (rt + 1) * part_rows, side * lanes : (side + 1) * lanes] = (
                        found.astype(BF)
                    )
                block = vall[slab, a, :, 0:width]
                values += [block, block]
            right = jnp.concatenate(values, axis=0)
            for ct in range(ct_n):
                ga[ct, 0:size_top, :] += jnp.dot(
                    sbuf[...], right[:, ct * TILE : (ct + 1) * TILE], preferred_element_type=F32
                )
            return 0

        lax.fori_loop(0, nhead // 2, pair, 0)

    add_slab(p)
    onward = []
    for dx, dh, copy in to_x:
        copy.wait()
        block = vall.at[pos_of(p, dx), head_of(dh)]
        copy = remote(block, block, s3.at[dx, dh], r3.at[dx, dh], partner)
        copy.start()
        onward.append(copy)
    for copy in to_mate:
        copy.wait()
    add_slab(mate)
    for dx in range(1, nx):
        add_slab(pos_of(p, dx))
    for copy in onward:
        copy.wait()
    for dx in range(1, nx):
        add_slab(pos_of(mate, dx))

    grads = [ga, gb]
    for n in reversed(range(layers)):
        now, later = grads[(top - n) % 2], grads[(top - n + 1) % 2]
        size = rows + 2 * wide[n]
        size_out = rows + 2 * outs[n]
        shift = wide[n] - outs[n]

        def lower(r, _):
            at_rows = pl.ds(pl.multiple_of(r * STEP, STEP), STEP)
            for ct in range(ct_n):
                gradbf[ct, at_rows, :] = now[ct, at_rows, :].astype(BF)
            return 0

        lax.fori_loop(0, size // STEP, lower, 0)
        loads["expand", n].wait()

        def middle(jt, _):
            js = pl.ds(pl.multiple_of(jt * TILE, TILE), TILE)
            total = None
            for ct in range(ct_n):
                term = lax.dot_general(
                    gradbf[ct, 0:size, :], expand[n, js, ct * TILE : (ct + 1) * TILE], NT,
                    preferred_element_type=F32,
                )
                total = term if total is None else total + term
            mp[jt, 0:size, :] = total
            ms[n, jt, 0:size, :] = total.astype(BF)
            mid_copy(n, jt).start()
            return 0

        lax.fori_loop(0, jt_n, middle, 0)
        if n == top:
            make_pre(0, True)

        def steepness(r, _):
            from_rows = pl.ds(pl.multiple_of(r * STEP, STEP) + (saved[n] - outs[n]) // STEP * STEP, STEP)
            at_rows = pl.ds(pl.multiple_of(r * STEP, STEP), STEP)
            for ct in range(ct_n):
                value = sv[n][from_rows, ct * TILE : (ct + 1) * TILE].astype(F32)
                ss[ct, at_rows, :] = gelu_slope(value)
            return 0

        skew = (saved[n] - outs[n]) % STEP
        lax.fori_loop(0, up(size_out + skew, STEP) // STEP, steepness, 0)
        for jt in range(jt_n):
            pre_copy(n, jt).wait()

        def slope_of_pre(r, _):
            at_rows = pl.ds(pl.multiple_of(r * STEP, STEP), STEP)
            keep = inside(r * STEP - wide[n], STEP)
            for jt in range(jt_n):
                value = pp[n, jt, at_rows, :] + pr[n, jt, at_rows, :].astype(F32)
                sp[jt, at_rows, :] = jnp.where(keep, gelu_slope(value), 0.0)
            return 0

        lax.fori_loop(0, size // STEP, slope_of_pre, 0)

        for jt in range(jt_n):
            mid_copy(n, jt).wait()
            gpf[0:size, :] = (mp[jt, 0:size, :] + mr[n, jt, 0:size, :].astype(F32)) * sp[jt, 0:size, :]
            for t in range(taps):
                begin = shift + (1 - t) * dil[n]
                gpw[t, 0:size_out, :] = gpf[begin : begin + size_out, :].astype(BF)

            def back(ct, _):
                at_channels = pl.ds(pl.multiple_of(ct * TILE, TILE), TILE)
                total = None
                for t in range(taps):
                    term = lax.dot_general(
                        gpw[t, 0:size_out, :], conv[n, t, at_channels, jt * TILE : (jt + 1) * TILE], NT,
                        preferred_element_type=F32,
                    )
                    total = term if total is None else total + term
                if jt == 0:
                    acc[ct, 0:size_out, :] = total
                else:
                    acc[ct, 0:size_out, :] += total
                return 0

            lax.fori_loop(0, ct_n, back, 0)

        def step_on(r, _):
            at_rows = pl.ds(pl.multiple_of(r * STEP, STEP), STEP)
            from_rows = pl.ds(pl.multiple_of(r * STEP + shift, 8), STEP)
            slope_rows = pl.ds(pl.multiple_of(r * STEP + skew, 8), STEP)
            for ct in range(ct_n):
                total = now[ct, from_rows, :] + acc[ct, at_rows, :] * ss[ct, slope_rows, :]
                if n:
                    later[ct, at_rows, :] = total
                else:
                    out_ref[at_rows, ct * TILE : (ct + 1) * TILE] = total.astype(BF)
            return 0

        lax.fori_loop(0, size_out // STEP, step_on, 0)


def per_device(
    inputs_saved,
    conv_weight,
    expand_weight,
    head_weight,
    batch_of,
    erase_left,
    erase_right,
    bin_gradient,
    cover_bins,
):
    npos, nhead = lax.axis_size("pos"), lax.axis_size("head")
    chan_place = lax.axis_index("chan")
    layers, rows, width = inputs_saved.shape
    taps, inner = conv_weight.shape[1], conv_weight.shape[3]
    exps, cover = cover_bins.shape

    projected = jnp.dot(head_weight, erase_left, preferred_element_type=F32)
    columns = jnp.arange(erase_left.shape[1]) // RANK
    chosen = (columns[None, :] == batch_of[:, None]).astype(F32)
    right_share = lax.dynamic_slice_in_dim(erase_right, chan_place * width, width, 0)
    weight_share = lax.dynamic_slice_in_dim(head_weight, chan_place * width, width, 1)
    removed_rows = jnp.dot(
        projected * chosen, right_share.astype(F32).T, precision=lax.Precision.HIGHEST
    )
    vectors = (weight_share.astype(F32) - removed_rows).astype(BF)

    def fold(array):
        return array.astype(BF).T.reshape(2, cover // 2, exps).transpose(1, 0, 2).reshape(cover // 2, 2 * exps)

    words = jnp.concatenate(
        [fold(cover_bins // 256), fold(cover_bins % 256), fold(bin_gradient), jnp.zeros((exps - 3 * cover // 2, 2 * exps), BF)]
    )
    pay = jnp.concatenate([vectors, words], axis=1)

    wide, _, saved = frames(layers)
    most = rows + 2 * wide[-1]
    span = rows + 2 * saved[-1]
    ct_n, jt_n = width // TILE, inner // TILE
    nx = npos // 2
    sems = pltpu.SemaphoreType.DMA
    return pl.pallas_call(
        functools.partial(kernel, layers, rows, width, inner, taps, npos, nhead, exps),
        out_shape=jax.ShapeDtypeStruct((rows, width), BF),
        in_specs=[pl.BlockSpec(memory_space=pl.ANY)] * 4,
        out_specs=pl.BlockSpec(memory_space=pltpu.VMEM),
        scratch_shapes=[
            *[pltpu.VMEM((rows + 2 * k, width), BF) for k in saved],
            pltpu.VMEM(conv_weight.shape, BF),
            pltpu.VMEM(expand_weight.shape, BF),
            pltpu.VMEM((npos, nhead, *pay.shape), BF),
            pltpu.VMEM((most, 4 * exps), BF),
            pltpu.VMEM((ct_n, span, TILE), F32),
            pltpu.VMEM((taps * ct_n, most, TILE), BF),
            pltpu.VMEM((layers, jt_n, most, TILE), F32),
            pltpu.VMEM((layers, jt_n, most, TILE), BF),
            pltpu.VMEM((layers, jt_n, most, TILE), BF),
            pltpu.VMEM((jt_n, most, TILE), F32),
            pltpu.VMEM((layers, jt_n, most, TILE), BF),
            pltpu.VMEM((layers, jt_n, most, TILE), BF),
            pltpu.VMEM((jt_n, most, TILE), F32),
            pltpu.VMEM((ct_n, most, TILE), F32),
            pltpu.VMEM((ct_n, most, TILE), F32),
            pltpu.VMEM((ct_n, most, TILE), F32),
            pltpu.VMEM((ct_n, most, TILE), F32),
            pltpu.VMEM((ct_n, most, TILE), BF),
            pltpu.VMEM((most, TILE), F32),
            pltpu.VMEM((taps, most, TILE), BF),
            sems((3 * layers,)),
            sems,
            sems((layers, 2)), sems((layers, 2)),
            sems((nhead,)), sems((nhead,)),
            sems((nhead,)), sems((nhead,)),
            sems((nx, nhead)), sems((nx, nhead)),
            sems((nx, nhead)), sems((nx, nhead)),
            sems((layers, jt_n)), sems((layers, jt_n)),
            sems((layers, jt_n)), sems((layers, jt_n)),
        ],
        compiler_params=pltpu.CompilerParams(
            collective_id=0, has_side_effects=True, vmem_limit_bytes=63 * 2**20
        ),
    )(inputs_saved, conv_weight, expand_weight, pay)


def solution(mesh):
    return jax.shard_map(
        per_device,
        mesh=mesh,
        in_specs=(
            P(None, ("pos", "head"), "chan"),
            P(None, None, "chan", None),
            P(None, None, "chan"),
            P(("pos", "head"), None),
            P(("pos", "head")),
            P(),
            P(),
            P(("pos", "head"), None),
            P(("pos", "head"), None),
        ),
        out_specs=P(("pos", "head"), "chan"),
        check_vma=False,
    )
```

time: 224 us -> 136 us (0.61)
  Pallas kernels: 0 us -> 126 us
  waiting for transfers between devices: 73.7 us -> 0 us
  blocking collectives: 48.6 us -> 0 us
  matrix products: 32.5 us -> 2.34 us
  other arithmetic: 20.1 us -> 1.4 us
  starting transfers between devices: 15.7 us -> 0 us
  local copies, waits for them, and re-layouts: 18.7 us -> 3.09 us
  between operations: 13.8 us -> 0.05 us
    pallas_call x0 -> x1, Pallas kernels: none -> 126 us  [per_device(): pl.pallas_call(functools.partial(kernel, layers, rows, width, inner, taps...]
    ppermute x8 -> x0, waiting for transfers between devices: 73.7 us -> none  [the longest x6 73.7 us: from_peer(): lax.ppermute(partial.astype(jnp.bfloat16), 'chan', pairs)]
    all_gather x1 -> x0, blocking collectives: 48.6 us -> none  [per_device(): entries = lax.all_gather(entries, SEQ, axis=2, tiled=True)]
    dot_general x18 -> x2, matrix products: 32.5 us -> 2.34 us  [the longest x1 1.21 us: per_device(): projected = jnp.dot(head_weight, erase_left, preferred_element_type=F32)]
    ppermute x8 -> x0, starting transfers between devices: 15.7 us -> none  [the longest x6 8.86 us: from_peer(): lax.ppermute(partial.astype(jnp.bfloat16), 'chan', pairs)]
    reduce_sum x1 -> x0, other arithmetic: 10.7 us -> none  [per_device(): jnp.sum(jnp.where(entries[0][:, None, :] == position[None, :, None], entr...]
    slice x15 -> x0, local copies, waits for them, and re-layouts: 9.5 us -> none  [the longest x1 7.28 us: per_device(): weight = conv_weight[n].reshape(taps * width, conv_weight.shape[3])]
    convert_element_type x7 -> x1, other arithmetic: 8.63 us -> 0.74 us  [fold(): array.astype(BF).T.reshape(2, cover // 2, exps).transpose(1, 0, 2)]
  transfers between devices with their start and end apart: 9 -> 0, of which waited for: 6 -> 0; matrix products, arithmetic and copies ran while one was open for 25% -> 0% of each run, Pallas kernels for 0% -> 0%
where the time goes in v2:
time: 136 us; the launch traced here: 133 us
  Pallas kernels  126 us (93%)
  local copies, waits for them, and re-layouts  3.09 us (2%)
  matrix products  2.34 us (2%)
  other arithmetic  1.4 us (1%)
    pallas_call x1, Pallas kernels, per_device(): pl.pallas_call(functools.partial(kernel, layers, rows, width, inner, taps...  126 us

profile of v2, /device:TPU:0, one launch (start us, length us, event | category | flops | bytes accessed | tf_op | source)
XLA Modules:
  0.0 133.1 jit_solution(5404613770484024183)
XLA Ops:
  0.0 0.0 copy-start
  0.0 0.7 copy.16
  0.8 0.1 reshape.37
  0.8 0.7 fusion.2
  1.6 0.1 reshape.33
  1.7 0.1 reshape.35
  1.8 1.2 convolution_select_fusion
  3.0 0.0 copy-done
  3.0 1.1 fusion
  4.2 0.7 maximum_maximum_fusion.pay_ref
  4.8 126.2 %shard_map.91 = bf16[512,768]{1,0:T(8,128)(2,1)} custom-call(bf16[3,512,768]{2,1,0:T(8,128)(2,1)} %inputs_ref.1, bf16[3,3,768,768]{3,2,1,0:T(8,128)(2,1)} %conv_ref.1, bf16[3,768,768]{2,1,0:T(8,128)(2,1)} %expand_ref.1, bf16[64,896]{1,0:T(8,128)(2,1)} %maximum_maximum_fusion.pay_ref), custom_call_target="tpu_custom_call" | custom-call | tf_op jit(solution)/shard_map/pallas_call | solution.py:399
  131.0 2.1 %copy.20 = bf16[512,768]{1,0:T(8,128)(2,1)} copy(bf16[512,768]{1,0:T(8,128)(2,1)} %shard_map.91) | data formatting | bytes 1572864
  (4 shorter events, 0.0 us)
Async XLA Ops:
  0.0 3.0 %copy-start = (bf16[1536,64]{0,1:T(8,128)(2,1)S(1)}, bf16[1536,64]{0,1:T(8,128)(2,1)}, u32[]{:S(2)}) copy-start(bf16[1536,64]{0,1:T(8,128)(2,1)} %param.15) | copy-start | bytes 589828

commit v3 on v2

v3 whole, which is shorter than its diff:
```python
import functools

import jax
import jax.numpy as jnp
from jax import lax
from jax.experimental import pallas as pl
from jax.experimental.pallas import tpu as pltpu
from jax.sharding import PartitionSpec as P

BASE_DILATION = 4
RANK = 8
SEQ = ("pos", "head")
MESH = pl.DeviceIdType.MESH
BF = jnp.bfloat16
F32 = jnp.float32
TILE = 256
STEP = 16
LANES = 128
STREAMS = 2
NT = (((1,), (1,)), ((), ()))


def gelu_value(value):
    return 0.5 * value * (1.0 + lax.erf(value * 0.7071067811865476))


def gelu_slope(value):
    return (
        0.5 * (1.0 + lax.erf(value * 0.7071067811865476))
        + value * jnp.exp(-0.5 * value * value) * 0.3989422804014327
    )


def up(value, unit):
    return -(-value // unit) * unit


def frames(layers):
    wide, out, saved, before = [], [], [], 0
    for n in range(layers):
        dilation = BASE_DILATION * 2**n
        out.append(before)
        before = up(before + dilation, 8)
        wide.append(before)
        saved.append(up(before + dilation, 16))
    return wide, out, saved


def kernel(
    layers, rows, width, inner, taps, npos, nhead, exps,
    inputs_ref, conv_ref, expand_ref, pay_ref,
    out_ref,
    sv0, sv1, sv2, conv, expand, vall, sbuf, actf, aw, pp, ps, pr, mp, ms, mr, go, gr,
    ss, top_grad, ga, gb, acc, gradbf, gpf,
    load_sem, own_sem, halo_s, halo_r, s1, r1, s2p, r2p, s2x, r2x, s3, r3,
    ps_s, ps_r, ms_s, ms_r, go_s, go_r,
):
    sv = [sv0, sv1, sv2]
    wide, outs, saved = frames(layers)
    dil = [BASE_DILATION * 2**n for n in range(layers)]
    members = npos * nhead
    p, h = lax.axis_index("pos"), lax.axis_index("head")
    mine = lax.axis_index("chan")
    peer = {"chan": 1 - mine}
    place = p * nhead + h
    after = lax.rem(place + 1, members)
    ahead = lax.rem(place + members - 1, members)
    follow = {"pos": after // nhead, "head": lax.rem(after, nhead)}
    precede = {"pos": ahead // nhead, "head": lax.rem(ahead, nhead)}
    mate = p + 1 - 2 * lax.rem(p, 2)
    partner = {"pos": mate}
    nx = npos // 2
    ct_n, half = width // TILE, inner // 2
    jt_n = half // LANES
    halves = [pl.multiple_of((1 - mine) * half, LANES), pl.multiple_of(mine * half, LANES)]

    def remote(src, dst, send, recv, device):
        return pltpu.make_async_remote_copy(
            src_ref=src, dst_ref=dst, send_sem=send, recv_sem=recv, device_id=device, device_id_type=MESH
        )

    def head_of(dh):
        return lax.rem(h + nhead - dh, nhead)

    def pos_of(start, dx):
        return lax.rem(start + npos - 2 * dx, npos)

    loads = {}
    at = 0
    for n in reversed(range(layers)):
        loads["saved", n] = [
            pltpu.make_async_copy(inputs_ref.at[n], sv[n].at[pl.ds(saved[n], rows)], load_sem.at[at])
        ]
        at += 1
        loads["conv", n], loads["expand", n] = [], []
        for side in range(2):
            for t in range(taps):
                loads["conv", n].append(
                    pltpu.make_async_copy(
                        conv_ref.at[n, t, :, pl.ds(halves[side], half)],
                        conv.at[n, side, :, pl.ds(t * half, half)],
                        load_sem.at[at],
                    )
                )
                at += 1
            loads["expand", n].append(
                pltpu.make_async_copy(
                    expand_ref.at[n, pl.ds(halves[side], half)], expand.at[n, side], load_sem.at[at]
                )
            )
            at += 1

    def load(kind, n):
        for copy in loads[kind, n]:
            copy.start()

    def loaded(kind, n):
        for copy in loads[kind, n]:
            copy.wait()

    own = pltpu.make_async_copy(pay_ref, vall.at[p, h], own_sem)
    own.start()
    load("saved", layers - 1)
    load("conv", layers - 1)

    barrier = pltpu.get_barrier_semaphore()
    known = [follow, precede, peer, partner]
    known += [{"head": lax.rem(h + dh, nhead)} for dh in range(1, nhead)]
    known += [{"pos": lax.rem(p + 2 * dx, npos)} for dx in range(1, nx)]
    for device in known:
        pl.semaphore_signal(barrier, inc=1, device_id=device, device_id_type=MESH)
    pl.semaphore_wait(barrier, len(known))

    halos = {}
    for n in reversed(range(layers)):
        k = saved[n]
        halos[n] = [
            remote(inputs_ref.at[n, pl.ds(rows - k, k)], sv[n].at[pl.ds(0, k)],
                   halo_s.at[n, 0], halo_r.at[n, 0], follow),
            remote(inputs_ref.at[n, pl.ds(0, k)], sv[n].at[pl.ds(rows + k, k)],
                   halo_s.at[n, 1], halo_r.at[n, 1], precede),
        ]
    for copy in halos[layers - 1]:
        copy.start()
    first = [
        remote(pay_ref, vall.at[p, h], s1.at[dh], r1.at[dh], {"head": lax.rem(h + dh, nhead)})
        for dh in range(1, nhead)
    ]
    for copy in first:
        copy.start()
    for n in reversed(range(layers - 1)):
        for copy in halos[n]:
            copy.start()
    for n in reversed(range(layers)):
        if n < layers - 1:
            load("saved", n)
            load("conv", n)
        load("expand", n)

    def inside(start, count, lanes):
        spot = place * rows + start + lax.broadcasted_iota(jnp.int32, (count, lanes), 0)
        return (spot >= 0) & (spot < members * rows)

    def make_pre(n):
        size = rows + 2 * wide[n]
        loaded("saved", n)
        for copy in halos[n]:
            copy.wait()

        def activate(r, _):
            place_at = pl.ds(pl.multiple_of(r * STEP, STEP), STEP)
            keep = inside(r * STEP - saved[n], STEP, TILE)
            for ct in range(ct_n):
                value = sv[n][place_at, ct * TILE : (ct + 1) * TILE].astype(F32)
                actf[ct, place_at, :] = jnp.where(keep, gelu_value(value), 0.0)
            return 0

        lax.fori_loop(0, (rows + 2 * saved[n]) // STEP, activate, 0)
        for t in range(taps):
            begin = saved[n] - wide[n] + (t - 1) * dil[n]
            for ct in range(ct_n):
                aw[t * ct_n + ct, 0:size, :] = actf[ct, begin : begin + size, :].astype(BF)
        loaded("conv", n)

        for side in range(2):
            total = None
            for t in range(taps):
                for ct in range(ct_n):
                    term = jnp.dot(
                        aw[t * ct_n + ct, 0:size, :],
                        conv[n, side, ct * TILE : (ct + 1) * TILE, t * half : (t + 1) * half],
                        preferred_element_type=F32,
                    )
                    total = term if total is None else total + term
            if side == 0:
                ps[n, 0:size, :] = total.astype(BF)
                pre_copy(n).start()
            else:
                pp[n, 0:size, :] = total

    def pre_copy(n):
        size = pl.ds(0, rows + 2 * wide[n])
        return remote(ps.at[n, size], pr.at[n, size], ps_s.at[n], ps_r.at[n], peer)

    def mid_copy(n, s, jt):
        size = pl.ds(0, part + 2 * wide[n])
        return remote(ms.at[n, s, jt, size], mr.at[n, s, jt, size], ms_s.at[n, s, jt], ms_r.at[n, s, jt], peer)

    def back_copy(n, s, jt):
        size = pl.ds(0, part + 2 * wide[n])
        return remote(go.at[n, s, jt, size], gr.at[n, s, jt, size], go_s.at[n, s, jt], go_r.at[n, s, jt], peer)

    part = rows // STREAMS
    top = layers - 1
    make_pre(top)

    own.wait()
    to_mate, to_x = [], []
    for dh in range(nhead):
        if dh:
            first[dh - 1].wait()
        block = vall.at[p, head_of(dh)]
        for dx in range(1, nx):
            copy = remote(block, block, s2x.at[dx, dh], r2x.at[dx, dh], {"pos": lax.rem(p + 2 * dx, npos)})
            copy.start()
            to_x.append((dx, dh, copy))
        copy = remote(block, block, s2p.at[dh], r2p.at[dh], partner)
        copy.start()
        to_mate.append(copy)

    if layers > 1:
        make_pre(top - 1)

    size_top = rows + 2 * wide[top]

    def clear(r, _):
        at_rows = pl.ds(pl.multiple_of(r * STEP, STEP), STEP)
        for ct in range(ct_n):
            top_grad[ct, at_rows, :] = jnp.zeros((STEP, TILE), F32)
        return 0

    lax.fori_loop(0, size_top // STEP, clear, 0)
    lanes = 2 * exps
    part_rows = size_top // 3

    def add_slab(slab):
        def pair(i, _):
            values = []
            for side in range(2):
                a = 2 * i + side
                words = vall[slab, a, :, width : width + lanes].astype(F32)
                spots = words[0:16] * 256.0 + words[16:32]
                heights = words[32:48]
                for rt in range(3):
                    line = (place * rows - wide[top] + rt * part_rows).astype(F32)
                    row = line + lax.broadcasted_iota(jnp.int32, (part_rows, lanes), 0).astype(F32)
                    found = jnp.zeros((part_rows, lanes), F32)
                    for k in range(16):
                        found = found + jnp.where(spots[k : k + 1] == row, heights[k : k + 1], 0.0)
                    sbuf[rt * part_rows : (rt + 1) * part_rows, side * lanes : (side + 1) * lanes] = (
                        found.astype(BF)
                    )
                block = vall[slab, a, :, 0:width]
                values += [block, block]
            right = jnp.concatenate(values, axis=0)
            for ct in range(ct_n):
                top_grad[ct, 0:size_top, :] += jnp.dot(
                    sbuf[...], right[:, ct * TILE : (ct + 1) * TILE], preferred_element_type=F32
                )
            return 0

        lax.fori_loop(0, nhead // 2, pair, 0)

    add_slab(p)
    onward = []
    for dx, dh, copy in to_x:
        copy.wait()
        block = vall.at[pos_of(p, dx), head_of(dh)]
        copy = remote(block, block, s3.at[dx, dh], r3.at[dx, dh], partner)
        copy.start()
        onward.append(copy)
    for copy in to_mate:
        copy.wait()
    add_slab(mate)
    for n in reversed(range(top - 1)):
        make_pre(n)
    for dx in range(1, nx):
        add_slab(pos_of(p, dx))
    for copy in onward:
        copy.wait()
    for dx in range(1, nx):
        add_slab(pos_of(mate, dx))

    grads = [ga, gb]

    def grad_of(n, s):
        if n == top:
            return lambda ct, start, count: top_grad[ct, pl.ds(s * part + start, count), :]
        held = grads[(top - n) % 2]
        return lambda ct, start, count: held[s, ct, pl.ds(start, count), :]

    def send_mid(n, s):
        size = part + 2 * wide[n]
        now = grad_of(n, s)
        for ct in range(ct_n):
            gradbf[ct, 0:size, :] = now(ct, 0, size).astype(BF)
        if s == 0:
            loaded("expand", n)
        for jt in range(jt_n):
            total = None
            for ct in range(ct_n):
                term = lax.dot_general(
                    gradbf[ct, 0:size, :],
                    expand[n, 0, jt * LANES : (jt + 1) * LANES, ct * TILE : (ct + 1) * TILE],
                    NT, preferred_element_type=F32,
                )
                total = term if total is None else total + term
            ms[n, s, jt, 0:size, :] = total.astype(BF)
            mid_copy(n, s, jt).start()
        total = None
        for ct in range(ct_n):
            term = lax.dot_general(
                gradbf[ct, 0:size, :], expand[n, 1, :, ct * TILE : (ct + 1) * TILE],
                NT, preferred_element_type=F32,
            )
            total = term if total is None else total + term
        mp[s, 0:size, :] = total

    def slope_of_pre(n):
        pre_copy(n).wait()

        def body(r, _):
            at_rows = pl.ds(pl.multiple_of(r * STEP, STEP), STEP)
            keep = inside(r * STEP - wide[n], STEP, half)
            value = pp[n, at_rows, :] + pr[n, at_rows, :].astype(F32)
            pp[n, at_rows, :] = jnp.where(keep, gelu_slope(value), 0.0)
            return 0

        lax.fori_loop(0, (rows + 2 * wide[n]) // STEP, body, 0)

    def slope_of_saved(n):
        base = (saved[n] - outs[n]) // STEP * STEP

        def body(r, _):
            from_rows = pl.ds(pl.multiple_of(r * STEP + base, STEP), STEP)
            at_rows = pl.ds(pl.multiple_of(r * STEP, STEP), STEP)
            for ct in range(ct_n):
                value = sv[n][from_rows, ct * TILE : (ct + 1) * TILE].astype(F32)
                ss[ct, at_rows, :] = gelu_slope(value)
            return 0

        skew = (saved[n] - outs[n]) % STEP
        lax.fori_loop(0, up(rows + 2 * outs[n] + skew, STEP) // STEP, body, 0)

    def send_back(n, s):
        size = part + 2 * wide[n]
        for jt in range(jt_n):
            lanes_at = slice(jt * LANES, (jt + 1) * LANES)
            mid_copy(n, s, jt).wait()
            go[n, s, jt, 0:size, :] = (
                (mp[s, 0:size, lanes_at] + mr[n, s, jt, 0:size, :].astype(F32))
                * pp[n, s * part : s * part + size, lanes_at]
            ).astype(BF)
            back_copy(n, s, jt).start()

    def finish(n, s):
        size, size_out = part + 2 * wide[n], part + 2 * outs[n]
        shift = wide[n] - outs[n]
        begins = [shift + (1 - t) * dil[n] for t in range(taps)]
        for jt in range(jt_n):
            gpf[0:size, jt * LANES : (jt + 1) * LANES] = go[n, s, jt, 0:size, :].astype(F32)
        left = jnp.concatenate([gpf[k : k + size_out, :].astype(BF) for k in begins], axis=1)
        for ct in range(ct_n):
            acc[ct, 0:size_out, :] = lax.dot_general(
                left, conv[n, 1, ct * TILE : (ct + 1) * TILE, :], NT, preferred_element_type=F32
            )
        for jt in range(jt_n):
            back_copy(n, s, jt).wait()
            gpf[0:size, 0:LANES] = gr[n, s, jt, 0:size, :].astype(F32)
            left = jnp.concatenate([gpf[k : k + size_out, 0:LANES].astype(BF) for k in begins], axis=1)
            for ct in range(ct_n):
                right = jnp.concatenate(
                    [
                        conv[n, 0, ct * TILE : (ct + 1) * TILE, t * half + jt * LANES : t * half + (jt + 1) * LANES]
                        for t in range(taps)
                    ],
                    axis=1,
                )
                acc[ct, 0:size_out, :] += lax.dot_general(left, right, NT, preferred_element_type=F32)
        now = grad_of(n, s)
        later = grads[(top - n + 1) % 2]
        skew = (saved[n] - outs[n]) % STEP
        for ct in range(ct_n):
            total = now(ct, shift, size_out) + acc[ct, 0:size_out, :] * ss[ct, pl.ds(s * part + skew, size_out), :]
            if n:
                later[s, ct, 0:size_out, :] = total
            else:
                out_ref[s * part : (s + 1) * part, ct * TILE : (ct + 1) * TILE] = total.astype(BF)

    for s in range(STREAMS):
        send_mid(top, s)
    for n in reversed(range(layers)):
        slope_of_pre(n)
        for s in range(STREAMS):
            send_back(n, s)
        slope_of_saved(n)
        for s in range(STREAMS):
            finish(n, s)
            if n:
                send_mid(n - 1, s)


def per_device(
    inputs_saved,
    conv_weight,
    expand_weight,
    head_weight,
    batch_of,
    erase_left,
    erase_right,
    bin_gradient,
    cover_bins,
):
    npos, nhead = lax.axis_size("pos"), lax.axis_size("head")
    chan_place = lax.axis_index("chan")
    layers, rows, width = inputs_saved.shape
    taps, inner = conv_weight.shape[1], conv_weight.shape[3]
    exps, cover = cover_bins.shape

    projected = jnp.dot(head_weight, erase_left, preferred_element_type=F32)
    columns = jnp.arange(erase_left.shape[1]) // RANK
    chosen = (columns[None, :] == batch_of[:, None]).astype(F32)
    right_share = lax.dynamic_slice_in_dim(erase_right, chan_place * width, width, 0)
    weight_share = lax.dynamic_slice_in_dim(head_weight, chan_place * width, width, 1)
    removed_rows = jnp.dot(
        projected * chosen, right_share.astype(F32).T, precision=lax.Precision.HIGHEST
    )
    vectors = (weight_share.astype(F32) - removed_rows).astype(BF)

    def fold(array):
        return array.astype(BF).T.reshape(2, cover // 2, exps).transpose(1, 0, 2).reshape(cover // 2, 2 * exps)

    words = jnp.concatenate(
        [fold(cover_bins // 256), fold(cover_bins % 256), fold(bin_gradient), jnp.zeros((exps - 3 * cover // 2, 2 * exps), BF)]
    )
    pay = jnp.concatenate([vectors, words], axis=1)

    wide, _, saved = frames(layers)
    most = rows + 2 * wide[-1]
    span = rows + 2 * saved[-1]
    part = rows // STREAMS
    short = part + 2 * wide[-1]
    ct_n, half = width // TILE, inner // 2
    jt_n = half // LANES
    nx = npos // 2
    sems = pltpu.SemaphoreType.DMA
    return pl.pallas_call(
        functools.partial(kernel, layers, rows, width, inner, taps, npos, nhead, exps),
        out_shape=jax.ShapeDtypeStruct((rows, width), BF),
        in_specs=[pl.BlockSpec(memory_space=pl.ANY)] * 4,
        out_specs=pl.BlockSpec(memory_space=pltpu.VMEM),
        scratch_shapes=[
            *[pltpu.VMEM((rows + 2 * k, width), BF) for k in saved],
            pltpu.VMEM((layers, 2, width, taps * half), BF),
            pltpu.VMEM((layers, 2, half, width), BF),
            pltpu.VMEM((npos, nhead, *pay.shape), BF),
            pltpu.VMEM((most, 4 * exps), BF),
            pltpu.VMEM((ct_n, span, TILE), F32),
            pltpu.VMEM((taps * ct_n, most, TILE), BF),
            pltpu.VMEM((layers, most, half), F32),
            pltpu.VMEM((layers, most, half), BF),
            pltpu.VMEM((layers, most, half), BF),
            pltpu.VMEM((STREAMS, short, half), F32),
            pltpu.VMEM((layers, STREAMS, jt_n, short, LANES), BF),
            pltpu.VMEM((layers, STREAMS, jt_n, short, LANES), BF),
            pltpu.VMEM((layers, STREAMS, jt_n, short, LANES), BF),
            pltpu.VMEM((layers, STREAMS, jt_n, short, LANES), BF),
            pltpu.VMEM((ct_n, most, TILE), F32),
            pltpu.VMEM((ct_n, most, TILE), F32),
            pltpu.VMEM((STREAMS, ct_n, short, TILE), F32),
            pltpu.VMEM((STREAMS, ct_n, short, TILE), F32),
            pltpu.VMEM((ct_n, short, TILE), F32),
            pltpu.VMEM((ct_n, short, TILE), BF),
            pltpu.VMEM((short, half), F32),
            sems((layers * (3 + 2 * taps),)),
            sems,
            sems((layers, 2)), sems((layers, 2)),
            sems((nhead,)), sems((nhead,)),
            sems((nhead,)), sems((nhead,)),
            sems((nx, nhead)), sems((nx, nhead)),
            sems((nx, nhead)), sems((nx, nhead)),
            sems((layers,)), sems((layers,)),
            sems((layers, STREAMS, jt_n)), sems((layers, STREAMS, jt_n)),
            sems((layers, STREAMS, jt_n)), sems((layers, STREAMS, jt_n)),
        ],
        compiler_params=pltpu.CompilerParams(
            collective_id=0, has_side_effects=True, vmem_limit_bytes=63 * 2**20
        ),
    )(inputs_saved, conv_weight, expand_weight, pay)


def solution(mesh):
    return jax.shard_map(
        per_device,
        mesh=mesh,
        in_specs=(
            P(None, ("pos", "head"), "chan"),
            P(None, None, "chan", None),
            P(None, None, "chan"),
            P(("pos", "head"), None),
            P(("pos", "head")),
            P(),
            P(),
            P(("pos", "head"), None),
            P(("pos", "head"), None),
        ),
        out_specs=P(("pos", "head"), "chan"),
        check_vma=False,
    )
```

time: 136 us -> 111 us (0.82); the launches traced: 133 us -> 111 us
  Pallas kernels: 126 us -> 104 us
    pallas_call x1, Pallas kernels: 126 us -> 104 us  [per_device(): pl.pallas_call(functools.partial(kernel, layers, rows, width, inner, taps...]
where the time goes in v3:
time: 111 us
  Pallas kernels  104 us (94%)
  local copies, waits for them, and re-layouts  3.09 us (3%)
  matrix products  2.33 us (2%)
  other arithmetic  1.4 us (1%)
    pallas_call x1, Pallas kernels, per_device(): pl.pallas_call(functools.partial(kernel, layers, rows, width, inner, taps...  104 us

profile of v3, /device:TPU:0, one launch (start us, length us, event | category | flops | bytes accessed | tf_op | source)
XLA Modules:
  0.0 110.6 jit_solution(660752904505507380)
XLA Ops:
  0.0 0.0 copy-start
  0.0 0.7 copy.16
  0.8 0.1 reshape.37
  0.8 0.7 fusion.2
  1.6 0.1 reshape.33
  1.7 0.1 reshape.35
  1.8 1.2 %convolution_select_fusion = f32[64,64]{1,0:T(8,128)S(1)} fusion(bf16[64,1536]{1,0:T(8,128)(2,1)} %param.12, bf16[1536,64]{0,1:T(8,128)(2,1)} %param.14, s32[64]{0:T(128)S(1)} %and_select_fusion, s32[64]{0:T(128)} %param.13), kind=kOutput, calls=%fused_computation.2 | convolution fusion | flops 12591104 | bytes 410112 | tf_op jit(solution)/shard_map/dot_general | solution.py:430
  3.0 0.0 copy-done
  3.0 1.1 %fusion = bf16[64,768]{1,0:T(8,128)(2,1)S(1)} fusion(f32[64,64]{1,0:T(8,128)S(1)} %convolution_select_fusion, bf16[1536,64]{0,1:T(8,128)(2,1)S(1)} %copy-done, s32[]{:T(128)S(6)} %select_n.25, bf16[64,1536]{1,0:T(8,128)(2,1)} %param.12), kind=kOutput, calls=%fused_computation.1 | convolution fusion | flops 37896192 | bytes 328704 | tf_op jit(solution)/shard_map/dot_general | solution.py:435
  4.1 0.7 maximum_maximum_fusion.pay_ref
  4.8 103.7 %shard_map.91 = bf16[512,768]{1,0:T(8,128)(2,1)} custom-call(bf16[3,512,768]{2,1,0:T(8,128)(2,1)} %inputs_ref.1, bf16[3,3,768,768]{3,2,1,0:T(8,128)(2,1)} %conv_ref.1, bf16[3,768,768]{2,1,0:T(8,128)(2,1)} %expand_ref.1, bf16[64,896]{1,0:T(8,128)(2,1)} %maximum_maximum_fusion.pay_ref), custom_call_target="tpu_custom_call" | custom-call | tf_op jit(solution)/shard_map/pallas_call | solution.py:457
  108.5 2.1 %copy.20 = bf16[512,768]{1,0:T(8,128)(2,1)} copy(bf16[512,768]{1,0:T(8,128)(2,1)} %shard_map.91) | data formatting | bytes 1572864
  (4 shorter events, 0.0 us)
Async XLA Ops:
  0.0 3.0 %copy-start = (bf16[1536,64]{0,1:T(8,128)(2,1)S(1)}, bf16[1536,64]{0,1:T(8,128)(2,1)}, u32[]{:S(2)}) copy-start(bf16[1536,64]{0,1:T(8,128)(2,1)} %param.15) | copy-start | bytes 589828

commit v4 on v3

--- a/solution.py
+++ b/solution.py
@@ -202,13 +202,17 @@
         size = pl.ds(0, rows + 2 * wide[n])
         return remote(ps.at[n, size], pr.at[n, size], ps_s.at[n], ps_r.at[n], peer)
 
+    def chunk(frame, s):
+        first_row = s * part + 2 * frame if s else 0
+        return first_row, (s + 1) * part + 2 * frame - first_row
+
     def mid_copy(n, s, jt):
-        size = pl.ds(0, part + 2 * wide[n])
-        return remote(ms.at[n, s, jt, size], mr.at[n, s, jt, size], ms_s.at[n, s, jt], ms_r.at[n, s, jt], peer)
+        at_rows = pl.ds(*chunk(wide[n], s))
+        return remote(ms.at[n, jt, at_rows], mr.at[n, jt, at_rows], ms_s.at[n, s, jt], ms_r.at[n, s, jt], peer)
 
     def back_copy(n, s, jt):
-        size = pl.ds(0, part + 2 * wide[n])
-        return remote(go.at[n, s, jt, size], gr.at[n, s, jt, size], go_s.at[n, s, jt], go_r.at[n, s, jt], peer)
+        at_rows = pl.ds(*chunk(wide[n], s))
+        return remote(go.at[n, jt, at_rows], gr.at[n, jt, at_rows], go_s.at[n, s, jt], go_r.at[n, s, jt], peer)
 
     part = rows // STREAMS
     top = layers - 1
@@ -291,19 +295,13 @@
     for dx in range(1, nx):
         add_slab(pos_of(mate, dx))
 
-    grads = [ga, gb]
-
-    def grad_of(n, s):
-        if n == top:
-            return lambda ct, start, count: top_grad[ct, pl.ds(s * part + start, count), :]
-        held = grads[(top - n) % 2]
-        return lambda ct, start, count: held[s, ct, pl.ds(start, count), :]
+    grads = [top_grad, ga, gb]
 
     def send_mid(n, s):
-        size = part + 2 * wide[n]
-        now = grad_of(n, s)
+        begin, size = chunk(wide[n], s)
+        at_rows = slice(begin, begin + size)
         for ct in range(ct_n):
-            gradbf[ct, 0:size, :] = now(ct, 0, size).astype(BF)
+            gradbf[ct, 0:size, :] = grads[top - n][ct, at_rows, :].astype(BF)
         if s == 0:
             loaded("expand", n)
         for jt in range(jt_n):
@@ -315,7 +313,7 @@
                     NT, preferred_element_type=F32,
                 )
                 total = term if total is None else total + term
-            ms[n, s, jt, 0:size, :] = total.astype(BF)
+            ms[n, jt, at_rows, :] = total.astype(BF)
             mid_copy(n, s, jt).start()
         total = None
         for ct in range(ct_n):
@@ -324,7 +322,7 @@
                 NT, preferred_element_type=F32,
             )
             total = term if total is None else total + term
-        mp[s, 0:size, :] = total
+        mp[at_rows, :] = total
 
     def slope_of_pre(n):
         pre_copy(n).wait()
@@ -353,49 +351,62 @@
         lax.fori_loop(0, up(rows + 2 * outs[n] + skew, STEP) // STEP, body, 0)
 
     def send_back(n, s):
-        size = part + 2 * wide[n]
+        begin, size = chunk(wide[n], s)
+        at_rows = slice(begin, begin + size)
         for jt in range(jt_n):
             lanes_at = slice(jt * LANES, (jt + 1) * LANES)
             mid_copy(n, s, jt).wait()
-            go[n, s, jt, 0:size, :] = (
-                (mp[s, 0:size, lanes_at] + mr[n, s, jt, 0:size, :].astype(F32))
-                * pp[n, s * part : s * part + size, lanes_at]
+            go[n, jt, at_rows, :] = (
+                (mp[at_rows, lanes_at] + mr[n, jt, at_rows, :].astype(F32)) * pp[n, at_rows, lanes_at]
             ).astype(BF)
             back_copy(n, s, jt).start()
 
+    def taps_of(n, s, source, jt):
+        begin, size = chunk(outs[n], s)
+        shift = wide[n] - outs[n]
+        low, high = begin + shift - dil[n], begin + shift + dil[n] + size
+        low, high = low // STEP * STEP, up(high, STEP)
+        gpf[0 : high - low, :] = source[n, jt, low:high, :].astype(F32)
+        starts = [begin + shift + (1 - t) * dil[n] - low for t in range(taps)]
+        return jnp.concatenate([gpf[k : k + size, :].astype(BF) for k in starts], axis=1)
+
+    def weights_of(n, side, ct, jt):
+        return jnp.concatenate(
+            [
+                conv[n, side, ct * TILE : (ct + 1) * TILE, t * half + jt * LANES : t * half + (jt + 1) * LANES]
+                for t in range(taps)
+            ],
+            axis=1,
+        )
+
+    def own_half(n, s):
+        begin, size = chunk(outs[n], s)
+        left = jnp.concatenate([taps_of(n, s, go, jt) for jt in range(jt_n)], axis=1)
+        for ct in range(ct_n):
+            right = jnp.concatenate([weights_of(n, 1, ct, jt) for jt in range(jt_n)], axis=1)
+            acc[ct, begin : begin + size, :] = lax.dot_general(left, right, NT, preferred_element_type=F32)
+
     def finish(n, s):
-        size, size_out = part + 2 * wide[n], part + 2 * outs[n]
-        shift = wide[n] - outs[n]
-        begins = [shift + (1 - t) * dil[n] for t in range(taps)]
-        for jt in range(jt_n):
-            gpf[0:size, jt * LANES : (jt + 1) * LANES] = go[n, s, jt, 0:size, :].astype(F32)
-        left = jnp.concatenate([gpf[k : k + size_out, :].astype(BF) for k in begins], axis=1)
-        for ct in range(ct_n):
-            acc[ct, 0:size_out, :] = lax.dot_general(
-                left, conv[n, 1, ct * TILE : (ct + 1) * TILE, :], NT, preferred_element_type=F32
-            )
+        begin, size = chunk(outs[n], s)
+        at_rows = slice(begin, begin + size)
         for jt in range(jt_n):
             back_copy(n, s, jt).wait()
-            gpf[0:size, 0:LANES] = gr[n, s, jt, 0:size, :].astype(F32)
-            left = jnp.concatenate([gpf[k : k + size_out, 0:LANES].astype(BF) for k in begins], axis=1)
+            left = taps_of(n, s, gr, jt)
             for ct in range(ct_n):
-                right = jnp.concatenate(
-                    [
-                        conv[n, 0, ct * TILE : (ct + 1) * TILE, t * half + jt * LANES : t * half + (jt + 1) * LANES]
-                        for t in range(taps)
-                    ],
-                    axis=1,
+                acc[ct, at_rows, :] += lax.dot_general(
+                    left, weights_of(n, 0, ct, jt), NT, preferred_element_type=F32
                 )
-                acc[ct, 0:size_out, :] += lax.dot_general(left, right, NT, preferred_element_type=F32)
-        now = grad_of(n, s)
-        later = grads[(top - n + 1) % 2]
+        shift = wide[n] - outs[n]
         skew = (saved[n] - outs[n]) % STEP
         for ct in range(ct_n):
-            total = now(ct, shift, size_out) + acc[ct, 0:size_out, :] * ss[ct, pl.ds(s * part + skew, size_out), :]
+            total = (
+                grads[top - n][ct, begin + shift : begin + shift + size, :]
+                + acc[ct, at_rows, :] * ss[ct, begin + skew : begin + skew + size, :]
+            )
             if n:
-                later[s, ct, 0:size_out, :] = total
+                grads[top - n + 1][ct, at_rows, :] = total
             else:
-                out_ref[s * part : (s + 1) * part, ct * TILE : (ct + 1) * TILE] = total.astype(BF)
+                out_ref[at_rows, ct * TILE : (ct + 1) * TILE] = total.astype(BF)
 
     for s in range(STREAMS):
         send_mid(top, s)
@@ -403,7 +414,10 @@
         slope_of_pre(n)
         for s in range(STREAMS):
             send_back(n, s)
+        own_half(n, 0)
         slope_of_saved(n)
+        for s in range(1, STREAMS):
+            own_half(n, s)
         for s in range(STREAMS):
             finish(n, s)
             if n:
@@ -470,18 +484,18 @@
             pltpu.VMEM((layers, most, half), F32),
             pltpu.VMEM((layers, most, half), BF),
             pltpu.VMEM((layers, most, half), BF),
-            pltpu.VMEM((STREAMS, short, half), F32),
-            pltpu.VMEM((layers, STREAMS, jt_n, short, LANES), BF),
-            pltpu.VMEM((layers, STREAMS, jt_n, short, LANES), BF),
-            pltpu.VMEM((layers, STREAMS, jt_n, short, LANES), BF),
-            pltpu.VMEM((layers, STREAMS, jt_n, short, LANES), BF),
+            pltpu.VMEM((most, half), F32),
+            pltpu.VMEM((layers, jt_n, most, LANES), BF),
+            pltpu.VMEM((layers, jt_n, most, LANES), BF),
+            pltpu.VMEM((layers, jt_n, most, LANES), BF),
+            pltpu.VMEM((layers, jt_n, most, LANES), BF),
             pltpu.VMEM((ct_n, most, TILE), F32),
             pltpu.VMEM((ct_n, most, TILE), F32),
-            pltpu.VMEM((STREAMS, ct_n, short, TILE), F32),
-            pltpu.VMEM((STREAMS, ct_n, short, TILE), F32),
-            pltpu.VMEM((ct_n, short, TILE), F32),
+            pltpu.VMEM((ct_n, most, TILE), F32),
+            pltpu.VMEM((ct_n, most, TILE), F32),
+            pltpu.VMEM((ct_n, most, TILE), F32),
             pltpu.VMEM((ct_n, short, TILE), BF),
-            pltpu.VMEM((short, half), F32),
+            pltpu.VMEM((most, LANES), F32),
             sems((layers * (3 + 2 * taps),)),
             sems,
             sems((layers, 2)), sems((layers, 2)),

time: 111 us -> 107 us (0.964)
  Pallas kernels: 104 us -> 99.9 us
    pallas_call x1, Pallas kernels: 104 us -> 99.9 us  [per_device(): pl.pallas_call(functools.partial(kernel, layers, rows, width, inner, taps...]
where the time goes in v4:
time: 107 us
  Pallas kernels  99.9 us (93%)
  local copies, waits for them, and re-layouts  3.09 us (3%)
  matrix products  2.33 us (2%)
  other arithmetic  1.4 us (1%)
    pallas_call x1, Pallas kernels, per_device(): pl.pallas_call(functools.partial(kernel, layers, rows, width, inner, taps...  99.9 us

profile of v4, /device:TPU:0, one launch (start us, length us, event | category | flops | bytes accessed | tf_op | source)
XLA Modules:
  0.0 106.7 jit_solution(6866332359969813719)
XLA Ops:
  0.0 0.0 copy-start
  0.0 0.7 copy.16
  0.8 0.1 reshape.37
  0.8 0.7 fusion.2
  1.6 0.1 reshape.33
  1.7 0.1 reshape.35
  1.8 1.2 %convolution_select_fusion = f32[64,64]{1,0:T(8,128)S(1)} fusion(bf16[64,1536]{1,0:T(8,128)(2,1)} %param.12, bf16[1536,64]{0,1:T(8,128)(2,1)} %param.14, s32[64]{0:T(128)S(1)} %and_select_fusion, s32[64]{0:T(128)} %param.13), kind=kOutput, calls=%fused_computation.2 | convolution fusion | flops 12591104 | bytes 410112 | tf_op jit(solution)/shard_map/dot_general | solution.py:444
  3.0 0.0 copy-done
  3.0 1.1 %fusion = bf16[64,768]{1,0:T(8,128)(2,1)S(1)} fusion(f32[64,64]{1,0:T(8,128)S(1)} %convolution_select_fusion, bf16[1536,64]{0,1:T(8,128)(2,1)S(1)} %copy-done, s32[]{:T(128)S(6)} %select_n.25, bf16[64,1536]{1,0:T(8,128)(2,1)} %param.12), kind=kOutput, calls=%fused_computation.1 | convolution fusion | flops 37896192 | bytes 328704 | tf_op jit(solution)/shard_map/dot_general | solution.py:449
  4.1 0.7 maximum_maximum_fusion.pay_ref
  4.8 99.9 %shard_map.91 = bf16[512,768]{1,0:T(8,128)(2,1)} custom-call(bf16[3,512,768]{2,1,0:T(8,128)(2,1)} %inputs_ref.1, bf16[3,3,768,768]{3,2,1,0:T(8,128)(2,1)} %conv_ref.1, bf16[3,768,768]{2,1,0:T(8,128)(2,1)} %expand_ref.1, bf16[64,896]{1,0:T(8,128)(2,1)} %maximum_maximum_fusion.pay_ref), custom_call_target="tpu_custom_call" | custom-call | tf_op jit(solution)/shard_map/pallas_call | solution.py:471
  104.7 2.1 %copy.20 = bf16[512,768]{1,0:T(8,128)(2,1)} copy(bf16[512,768]{1,0:T(8,128)(2,1)} %shard_map.91) | data formatting | bytes 1572864
  (4 shorter events, 0.0 us)
Async XLA Ops:
  0.0 3.0 %copy-start = (bf16[1536,64]{0,1:T(8,128)(2,1)S(1)}, bf16[1536,64]{0,1:T(8,128)(2,1)}, u32[]{:S(2)}) copy-start(bf16[1536,64]{0,1:T(8,128)(2,1)} %param.15) | copy-start | bytes 589828
